TPU v7x, 32 devices: a whole 2x2x4 slice. The times are simulated.
32 devices in a mesh: groups: 2 (over x), dp: 2 (over core), tensor: 8 (over z, y).
Axes of the slice: x: 2, y: 2, z: 4, core: 2. Of those that a mesh axis runs over, the one named last changes fastest.
Arguments:
- suffix_acts: bfloat16 [4, 768, 4096], P(('groups', 'dp'), 'tensor'), parts along dimension 0, may hold values from -6 to 6
- suffix_lens: int32 [4, 16], P(('groups', 'dp')), parts along dimension 0, may hold values from 8 to 48, as said below
- hit_holder: int32 [4, 16], P('groups'), parts along dimension 0, may hold values from 0 to 1
- hit_slot: int32 [4, 16], P('groups'), parts along dimension 0, may hold values from 0 to 15
- cache_states: float32 [64, 128, 64, 128], P(('groups', 'dp'), 'tensor'), parts along dimension 0, may hold values from -0.8 to 0.8
- cache_conv_x: bfloat16 [64, 3, 8192], P(('groups', 'dp'), None, 'tensor'), parts along dimension 0, may hold values from -6 to 6
- cache_conv_bc: bfloat16 [64, 3, 1024], P(('groups', 'dp'), None, 'tensor'), parts along dimension 0, may hold values from -6 to 6
- w_in_x: bfloat16 [4096, 8192], P(None, 'tensor'), may hold values from -0.09375 to 0.09375
- w_in_z: bfloat16 [4096, 8192], P(None, 'tensor'), may hold values from -0.09375 to 0.09375
- w_in_bc: bfloat16 [4096, 1024], P(None, 'tensor'), may hold values from -0.09375 to 0.09375
- w_in_dt: bfloat16 [4096, 128], P(None, 'tensor'), may hold values from -0.09375 to 0.09375
- conv_x: float32 [4, 8192], P(None, 'tensor'), may hold values from -3 to 3
- conv_bc: float32 [4, 1024], P(None, 'tensor'), may hold values from -3 to 3
- dt_bias: float32 [128], P('tensor'), may hold values from -2 to 0.5
- decay_rate: float32 [128], P('tensor'), may hold values from 0.004 to 0.15
- skip_gain: float32 [128], P('tensor'), may hold values from 0.5 to 1.5
- norm_gain: float32 [8192], P('tensor'), may hold values from 0.5 to 1.5
- w_out: bfloat16 [8192, 4096], P('tensor'), may hold values from -0.0625 to 0.0625
Outputs:
- mixed_out: bfloat16 [4, 768, 4096], P(('groups', 'dp'), 'tensor'), parts along dimension 0
- new_states: float32 [4, 16, 128, 64, 128], P(('groups', 'dp'), None, 'tensor'), parts along dimension 0
- new_tail_x: bfloat16 [4, 16, 3, 8192], P(('groups', 'dp'), None, None, 'tensor'), parts along dimension 0
- new_tail_bc: bfloat16 [4, 16, 3, 1024], P(('groups', 'dp'), None, None, 'tensor'), parts along dimension 0
There are 2 independent parts, one for each index of `groups`. A program takes and returns all parts, laid end to end along the dimension named above; an argument that names none is the same for every part. Nothing has to cross between parts.
Inputs may be any that keep to these rules, and one draw needn't show every extreme that they name: `suffix_lens`: every replica has a request of exactly 48 suffix tokens and one of 8.
All inputs are finite; a program needn't handle non-finite values.
Results may differ from a plain program's by a relative error of at most 0.0077.
Values may be sent and summed in bfloat16 or wider, within the bound.
A program may use at most 192 MiB of HBM per device.

v0:
```python
import jax
import jax.numpy as jnp
from jax import lax
from jax.sharding import PartitionSpec as P

HEADS = 128
HDIM = 64
NSTATE = 128
GROUPS = 4
KT = 3


highest = lax.Precision.HIGHEST
epsilon = 1e-05


def causal_conv(tail_rows, raw_rows, weight):
    extended = jnp.concatenate([tail_rows, raw_rows], axis=-2)
    seq_len = raw_rows.shape[-2]
    running = jnp.zeros(raw_rows.shape, jnp.float32)
    for offset in range(weight.shape[0]):
        running = running + weight[offset] * extended[..., offset : offset + seq_len, :].astype(
            jnp.float32
        )
    return (extended, lax.optimization_barrier(jax.nn.silu(running).astype(jnp.bfloat16)))


def last_rows(extended, lengths):
    index_rows = lengths[..., None] + jnp.arange(KT, dtype=jnp.int32)
    return jnp.take_along_axis(extended, index_rows[..., None], axis=-2)


def scan_block(values, scores, b_rows, c_rows, step_size, decay_rate, start_state, skip_gain):
    log_step = -decay_rate * step_size
    log_sum = jnp.cumsum(log_step, axis=-2)
    position = jnp.arange(values.shape[-3], dtype=jnp.int32)
    causal = position[:, None] >= position[None, :]
    log_gap = log_sum[..., :, None, :] - log_sum[..., None, :, :]
    decay_mat = jnp.where(causal[:, :, None], jnp.exp(jnp.minimum(log_gap, 0.0)), 0.0)
    weights = scores * decay_mat * step_size[..., None, :, :]
    outputs = jnp.einsum("...tsh,...shp->...thp", weights, values, precision=highest)
    carried = jnp.einsum("...thn,...hpn->...thp", c_rows, start_state, precision=highest)
    outputs = outputs + jnp.exp(log_sum)[..., None] * carried + skip_gain[:, None] * values
    weight_tail = jnp.exp(log_sum[..., -1:, :] - log_sum) * step_size
    scaled_vals = weight_tail[..., None] * values
    end_state = jnp.exp(log_sum[..., -1, :])[..., None, None] * start_state
    end_state = end_state + jnp.einsum(
        "...shp,...shn->...hpn", scaled_vals, b_rows, precision=highest
    )
    return (outputs, end_state)


def local(
    suffix_acts,
    suffix_lens,
    hit_holder,
    hit_slot,
    cache_states,
    cache_conv_x,
    cache_conv_bc,
    w_in_x,
    w_in_z,
    w_in_bc,
    w_in_dt,
    conv_x,
    conv_bc,
    dt_bias,
    decay_rate,
    skip_gain,
    norm_gain,
    w_out,
):
    replica = lax.axis_index("dp")
    lengths = suffix_lens[0]
    requests = lengths.shape[0]
    from_me = hit_holder == replica
    keep_mask = from_me[:, :, None, None]
    send_state = jnp.where(from_me[:, :, None, None, None], cache_states[hit_slot], 0.0)
    send_x = jnp.where(keep_mask, cache_conv_x[hit_slot].astype(jnp.float32), 0.0)
    send_bc = jnp.where(keep_mask, cache_conv_bc[hit_slot].astype(jnp.float32), 0.0)
    got_state, got_x, got_bc = (
        lax.all_to_all(send_state, "dp", split_axis=0, concat_axis=0, tiled=True),
        lax.all_to_all(send_x, "dp", split_axis=0, concat_axis=0, tiled=True),
        lax.all_to_all(send_bc, "dp", split_axis=0, concat_axis=0, tiled=True),
    )
    start_state = jnp.sum(got_state, axis=0)
    tail_x = jnp.sum(got_x, axis=0).astype(jnp.bfloat16)
    tail_bc = jnp.sum(got_bc, axis=0).astype(jnp.bfloat16)
    local_x = w_in_x.shape[1]
    local_bc = w_in_bc.shape[1]
    local_heads = w_in_dt.shape[1]
    flat_rows = lax.all_gather(suffix_acts, "tensor", axis=1, tiled=True)[0]
    pieces = [
        jnp.dot(flat_rows, w_in_x, preferred_element_type=jnp.float32),
        jnp.dot(flat_rows, w_in_z, preferred_element_type=jnp.float32),
        jnp.dot(flat_rows, w_in_bc, preferred_element_type=jnp.float32),
        jnp.dot(flat_rows, w_in_dt, preferred_element_type=jnp.float32),
    ]
    projected = jnp.concatenate(pieces, axis=-1)[None]
    projected = projected[0].reshape(requests, -1, projected.shape[-1])
    seq_len = projected.shape[1]
    raw_x = projected[..., :local_x].astype(jnp.bfloat16)
    raw_z = projected[..., local_x : 2 * local_x].astype(jnp.bfloat16)
    raw_bc = projected[..., 2 * local_x : 2 * local_x + local_bc].astype(jnp.bfloat16)
    raw_x, raw_z, raw_bc = lax.optimization_barrier((raw_x, raw_z, raw_bc))
    raw_dt = projected[..., 2 * local_x + local_bc :]
    ext_x, act_x = causal_conv(tail_x, raw_x, conv_x)
    ext_bc, act_bc = causal_conv(tail_bc, raw_bc, conv_bc)
    new_tail_x = last_rows(ext_x, lengths)
    new_tail_bc = last_rows(ext_bc, lengths)
    every_bc = lax.all_gather(act_bc, "tensor", axis=2, tiled=True)
    half_width = GROUPS * NSTATE
    b_all = every_bc[..., :half_width].reshape(requests, seq_len, GROUPS, NSTATE)
    c_all = every_bc[..., half_width:].reshape(requests, seq_len, GROUPS, NSTATE)
    head_ids = lax.axis_index("tensor") * local_heads + jnp.arange(local_heads, dtype=jnp.int32)
    head_group = head_ids % GROUPS
    group_scores = jnp.einsum("qtgn,qsgn->qtsg", c_all, b_all, preferred_element_type=jnp.float32)
    scores = jnp.take(group_scores, head_group, axis=3)
    b_heads = jnp.take(b_all, head_group, axis=2).astype(jnp.float32)
    c_heads = jnp.take(c_all, head_group, axis=2).astype(jnp.float32)
    live = jnp.arange(seq_len, dtype=jnp.int32)[None, :] < lengths[:, None]
    step_size = jnp.where(live[..., None], jax.nn.softplus(raw_dt + dt_bias), 0.0)
    values = act_x.astype(jnp.float32).reshape(requests, seq_len, local_heads, HDIM)
    outputs, new_states = scan_block(
        values, scores, b_heads, c_heads, step_size, decay_rate, start_state, skip_gain
    )
    gated = outputs * jax.nn.silu(raw_z.astype(jnp.float32)).reshape(
        requests, seq_len, local_heads, HDIM
    )
    per_head = jnp.sum(gated * gated, axis=-1)
    member = (head_group[:, None] == jnp.arange(GROUPS, dtype=jnp.int32)[None, :]).astype(
        jnp.float32
    )
    group_part = jnp.sum(per_head[..., :, None] * member, axis=-2)
    group_total = lax.psum(group_part, "tensor")
    mean_square = jnp.sum(group_total[..., None, :] * member, axis=-1) / (HEADS // GROUPS * HDIM)
    scaled = (
        gated * lax.rsqrt(mean_square + epsilon)[..., None] * norm_gain.reshape(local_heads, HDIM)
    )
    normed = (
        jnp.where(live[..., None, None], scaled, 0.0)
        .astype(jnp.bfloat16)
        .reshape(requests * seq_len, local_x)
    )
    mixed_out = lax.psum_scatter(
        jnp.dot(normed, w_out, preferred_element_type=jnp.float32),
        "tensor",
        scatter_dimension=0,
        tiled=True,
    )
    return (
        mixed_out.astype(jnp.bfloat16)[None],
        new_states[None],
        new_tail_x[None],
        new_tail_bc[None],
    )


def solution(mesh):
    return jax.shard_map(
        local,
        mesh=mesh,
        in_specs=(
            P(("groups", "dp"), "tensor", None),
            P(("groups", "dp"), None),
            P("groups", None),
            P("groups", None),
            P(("groups", "dp"), "tensor", None, None),
            P(("groups", "dp"), None, "tensor"),
            P(("groups", "dp"), None, "tensor"),
            P(None, "tensor"),
            P(None, "tensor"),
            P(None, "tensor"),
            P(None, "tensor"),
            P(None, "tensor"),
            P(None, "tensor"),
            P("tensor"),
            P("tensor"),
            P("tensor"),
            P("tensor"),
            P("tensor", None),
        ),
        out_specs=(
            P(("groups", "dp"), "tensor", None),
            P(("groups", "dp"), None, "tensor", None, None),
            P(("groups", "dp"), None, None, "tensor"),
            P(("groups", "dp"), None, None, "tensor"),
        ),
        check_vma=False,
    )
```

profile of v0, /device:TPU:0, one launch (start us, length us, event | category | flops | bytes accessed | tf_op | source)
XLA Modules:
  0.0 513.2 jit_solution(15891203723332577537)
XLA Ops:
  7.2 0.7 all-gather.3.cloned.1.call-update
  7.9 0.7 compare_select_fusion.3
  8.7 1.4 gather_fusion.1
  10.1 0.7 broadcast_compare_fusion
  10.8 0.7 copy_select_fusion.1
  11.5 3.3 all-to-all-start.1
  14.8 2.0 gather_fusion
  17.0 11.9 %gather_fusion.3 = f32[32,16,64,128]{3,2,1,0:T(8,128)} fusion(f32[16,16,64,128]{3,2,1,0:T(8,128)} %param.24, s32[1024]{0:T(1024)S(1)} %pad_clamp_fusion.2), kind=kCustom, calls=%fused_computation.5 | custom fusion | bytes 33554560 | tf_op jit(solution)/shard_map/gather | solution.py:78
  29.0 0.8 copy_select_fusion
  29.8 3.5 all-to-all-start
  33.3 12.4 %broadcast_select_fusion = f32[2,16,16,64,128]{4,3,2,1,0:T(8,128)} fusion(f32[2,16,16,64,128]{4,3,2,1,0:T(8,128)} %bitcast.77, pred[2,16]{1,0:T(4,128)(4,1)S(1)} %broadcast_compare_fusion), kind=kLoop, calls=%fused_computation.9 | loop fusion | flops 4194304 | bytes 33554464 | tf_op jit(solution)/shard_map/jit(_where)/select_n | solution.py:78
  45.7 9.7 %all-to-all-start.2 = ((f32[2,16,16,64,128]{4,3,2,1,0:T(8,128)}), f32[2,16,16,64,128]{4,3,2,1,0:T(8,128)}, u32[]{:S(2)}, u32[]{:S(2)}) async-start(f32[2,16,16,64,128]{4,3,2,1,0:T(8,128)} %broadcast_select_fusion), calls=%async_computation.2 | async-start | bytes 33554432 | tf_op jit(solution)/shard_map/all_to_all | solution.py:82
  55.5 13.5 %all-to-all-done.2 = f32[2,16,16,64,128]{4,3,2,1,0:T(8,128)} async-done(((f32[2,16,16,64,128]{4,3,2,1,0:T(8,128)}), f32[2,16,16,64,128]{4,3,2,1,0:T(8,128)}, u32[]{:S(2)}, u32[]{:S(2)}) %all-to-all-start.2) | async-done | bytes 16777248 | tf_op jit(solution)/shard_map/all_to_all | solution.py:82
  69.0 12.1 %reduce_sum.56 = f32[16,16,64,128]{3,2,1,0:T(8,128)} reduce(f32[2,16,16,64,128]{4,3,2,1,0:T(8,128)} %all-to-all-done.2, f32[]{:T(128)} %constant.84.clone.1), dimensions={0}, to_apply=%region_3.4 | reduce | flops 2097152 | bytes 25165828 | tf_op jit(solution)/shard_map/reduce_sum | solution.py:86
  81.3 30.7 %all-gather.3.cloned.1.call-done = bf16[1,768,4096]{2,1,0:T(8,128)(2,1)} async-done(((bf16[1,96,4096]{2,1,0:T(8,128)(2,1)}), bf16[1,768,4096]{2,1,0:T(8,128)(2,1)}) %all-gather.3.cloned.1.call-update) | async-done | bytes 6291472 | tf_op jit(solution)/shard_map/all_gather | solution.py:92
  112.0 12.3 %fusion.11 = f32[768,1024]{1,0:T(8,128)S(1)} fusion(bf16[4096,1024]{1,0:T(8,128)(2,1)} %param.27, bf16[1,768,4096]{2,1,0:T(8,128)(2,1)} %all-gather.3.cloned.1.call-done), kind=kOutput, calls=%fused_computation.26 | convolution fusion | flops 6442450944 | bytes 17825792 | tf_op jit(solution)/shard_map/dot_general | solution.py:94
  124.3 9.1 %fusion.9 = f32[768,1024]{1,0:T(8,128)S(1)} fusion(bf16[4096,1024]{1,0:T(8,128)(2,1)} %param.28, bf16[1,768,4096]{2,1,0:T(8,128)(2,1)S(1)} %copy-done.17), kind=kOutput, calls=%fused_computation.24 | convolution fusion | flops 6442450944 | bytes 17825792 | tf_op jit(solution)/shard_map/dot_general | solution.py:95
  133.5 1.8 fusion.5
  135.3 1.8 fusion.7
  137.1 0.6 pad_maximum_fusion
  137.7 3.8 copy.180
  141.5 1.6 fusion.51
  143.1 1.2 multiply_convert_fusion.1
  144.3 0.2 reduce-scatter.2.cloned.1.call-start
  144.6 10.0 %copy.117 = f32[16,48,2192]{2,0,1:T(8,128)} copy(f32[16,48,2192]{2,1,0:T(8,128)} %bitcast.79) | data formatting | bytes 13467648 | tf_op jit(solution)/shard_map/reshape;squeeze;broadcast_in_dim | solution.py:100
  154.6 2.8 multiply_convert_fusion
  157.4 5.3 %reshape.350 = bf16[16,48,16,64]{3,2,0,1:T(8,128)(2,1)} reshape(bf16[16,48,1024]{2,0,1:T(8,128)(2,1)} %multiply_convert_fusion) | data formatting | bytes 3145728 | tf_op jit(solution)/shard_map/reshape | solution.py:123
  162.6 1.4 fusion.31
  164.0 0.9 copy.129
  165.0 0.9 copy.127
  165.8 2.1 exponential_multiply_fusion
  167.9 0.9 copy.132
  168.8 2.5 convert_multiply_fusion.3
  171.3 5.7 %reshape.349 = f32[16,48,16,64]{3,2,0,1:T(8,128)} reshape(f32[16,48,1024]{2,0,1:T(8,128)} %convert_multiply_fusion.3) | data formatting | bytes 6291456 | tf_op jit(solution)/shard_map/reshape | solution.py:127
  177.0 10.9 %all-gather.5.cloned.1.call-done = bf16[16,48,1024]{2,0,1:T(8,128)(2,1)} async-done(((bf16[16,48,128]{2,0,1:T(8,128)(2,1)}), bf16[16,48,1024]{2,0,1:T(8,128)(2,1)}) %all-gather.5.cloned.1.call-update) | async-done | bytes 1572880 | tf_op jit(solution)/shard_map/all_gather | solution.py:111
  188.0 1.5 fusion.52
  189.5 0.2 reshape.348
  189.7 0.5 copy.123
  190.4 0.5 copy.122
  190.9 2.2 convolution_bitcast_fusion
  193.1 2.7 gather_fusion.6
  195.7 2.6 gather_fusion.7
  198.3 1.9 copy.124
  200.2 5.1 %select_bitcast_fusion = (bf16[16,48,16,128]{3,1,0,2:T(8,128)(2,1)}, bf16[16,48,16,128]{3,1,0,2:T(8,128)(2,1)S(1)}) fusion(bf16[16,16,48,128]{3,2,1,0:T(8,128)(2,1)} %gather_fusion.7, pred[16]{0:T(512)(128)(4,1)S(1)} %compare_and_fusion, bf16[16,16,48,128]{3,2,1,0:T(8,128)(2,1)} %gather_fusion.6), kind=kLoop, calls=%fused_computation.44 | loop fusion | flops 3145728 | bytes 12582928 | tf_op jit(solution)/shard_map/jit(_take)/select_n | solution.py:119
  205.3 11.0 %fusion.21 = f32[16,16,64,48]{2,3,1,0:T(8,128)} fusion(f32[16,16,64,128]{3,2,1,0:T(8,128)} %reduce_sum.56, bf16[16,48,16,128]{3,1,0,2:T(8,128)(2,1)S(1)} %get-tuple-element.42), kind=kOutput, calls=%fused_computation.42 | convolution fusion | flops 1207959552 | bytes 14680064 | tf_op jit(solution)/shard_map/...thn,...hpn->...thp/dot_general | solution.py:42
  216.4 3.6 gather_fusion.2
  220.0 20.2 %multiply_reduce_fusion = (f32[16,48,16]{1,2,0:T(8,128)S(1)}, f32[16,48,16,64]{3,1,2,0:T(8,128)}) fusion(f32[16,48,16,64]{3,2,0,1:T(8,128)} %reshape.349, bf16[16,48,16,64]{3,2,0,1:T(8,128)(2,1)} %reshape.350, f32[16]{0:T(128)S(1)} %copy-done.20, f32[16,16,64,48]{2,3,1,0:T(8,128)} %fusion.21, f32[16,48,16]{1,2,0:T(8,128)S(1)} %copy-done.10, ...), kind=kOutput, calls=%fused_computation.31 | convolution fusion | flops 462802944 | bytes 13568336 | tf_op jit(solution)/shard_map/...tsh,...shp->...thp/dot_general | solution.py:41
  240.3 34.6 %psum.7 = f32[16,48,4]{1,2,0:T(4,128)S(1)} all-reduce(f32[16,48,4]{1,2,0:T(4,128)S(1)} %multiply_reduce_fusion.2), channel_id=1, replica_groups=mesh['groups'=2,'dp'=2,'tensor'=8] {'tensor'}, use_global_device_ids=true, to_apply=%region_6.8 | all-reduce | flops 3072 | bytes 24576 | tf_op jit(solution)/shard_map/psum | solution.py:135
  275.1 4.5 select_convert_fusion
  279.7 2.5 copy.138
  282.1 4.5 reshape.270
  286.6 12.4 %fusion.54 = f32[768,4096]{1,0:T(8,128)} fusion(bf16[768,1024]{1,0:T(8,128)(2,1)S(1)} %reshape.270, bf16[1024,4096]{1,0:T(8,128)(2,1)} %param.37), kind=kOutput, calls=%fused_computation.120 | convolution fusion | flops 6442450944 | bytes 22544384 | tf_op jit(solution)/shard_map/dot_general | solution.py:146
  299.0 0.6 copy-done.13
  300.0 0.2 copy.139
  300.2 0.3 copy-done.4
  300.6 1.4 pad_maximum_fusion.1
  301.9 1.9 gather_fusion.4
  304.0 0.7 copy.142
  304.7 1.0 gather_fusion.5
  305.8 0.6 copy.143
  306.4 0.7 fusion.48
  307.1 16.1 %add_bitcast_fusion = f32[1,16,16,64,128]{4,3,2,1,0:T(8,128)} fusion(f32[16,16,64,128]{3,2,1,0:T(8,128)} %reduce_sum.56, f32[16,16]{1,0:T(8,128)S(1)} %fusion.48, bf16[16,48,16,128]{3,1,0,2:T(8,128)(2,1)} %get-tuple-element.41, f32[16,48,16]{1,2,0:T(8,128)S(1)} %copy.139, bf16[16,48,16,64]{3,2,0,1:T(8,128)(2,1)} %reshape.350), kind=kOutput, calls=%fused_computation.8 | convolution fusion | flops 1213726720 | bytes 21545984 | tf_op jit(solution)/shard_map/...shp,...shn->...hpn/dot_general | solution.py:47
  323.3 180.5 %reduce-scatter.2.cloned.1.call-done = f32[96,4096]{1,0:T(8,128)} async-done(((f32[768,4096]{1,0:T(8,128)}), f32[96,4096]{1,0:T(8,128)}) %reduce-scatter.2.cloned.1.call-update) | async-done | bytes 1572880 | tf_op jit(solution)/shard_map/reduce_scatter | solution.py:145
  503.8 2.4 convert_bitcast_fusion
  (78 shorter events, 2.0 us)
Async XLA Ops:
  7.2 128.1 %copy-start = (bf16[4096,128]{1,0:T(8,128)(2,1)S(1)}, bf16[4096,128]{1,0:T(8,128)(2,1)}, u32[]{:S(2)}) copy-start(bf16[4096,128]{1,0:T(8,128)(2,1)} %param.29) | copy-start | bytes 3145732
  7.2 9.6 %copy-start.12 = (s32[1,16]{1,0:T(1,128)S(1)}, s32[1,16]{1,0:T(1,128)}, u32[]{:S(2)}) copy-start(s32[1,16]{1,0:T(1,128)} %param.21) | copy-start | bytes 196
  7.2 9.8 %copy-start.19 = (f32[16]{0:T(128)S(1)}, f32[16]{0:T(128)}, u32[]{:S(2)}) copy-start(f32[16]{0:T(128)} %param.34) | copy-start | bytes 196
  7.2 104.8 %all-gather.3.cloned.1.call-start = ((), (), s32[]{:S(2)}) async-start(), calls=%async_computation.4 | async-start | bytes 7077888 | tf_op jit(solution)/shard_map/all_gather | solution.py:92
  11.5 18.4 %all-to-all-start.1 = ((f32[2,16,3,128]{3,1,2,0:T(8,128)}), f32[2,16,3,128]{3,1,2,0:T(8,128)S(1)}, u32[]{:S(2)}, u32[]{:S(2)}) async-start(f32[2,16,3,128]{3,1,2,0:T(8,128)} %copy_select_fusion.1), calls=%async_computation.1 | async-start | bytes 98304 | tf_op jit(solution)/shard_map/all_to_all | solution.py:84
  17.0 11.9 %copy-start.14 = (f32[1024]{0:T(1024)S(1)}, f32[1024]{0:T(1024)}, u32[]{:S(2)}) copy-start(f32[1024]{0:T(1024)} %param.36) | copy-start | bytes 12292
  29.8 15.9 %all-to-all-start = ((f32[2,16,3,1024]{3,1,2,0:T(8,128)}), f32[2,16,3,1024]{3,1,2,0:T(8,128)S(1)}, u32[]{:S(2)}, u32[]{:S(2)}) async-start(f32[2,16,3,1024]{3,1,2,0:T(8,128)} %copy_select_fusion), calls=%async_computation | async-start | bytes 786432 | tf_op jit(solution)/shard_map/all_to_all | solution.py:83
  45.7 23.3 %all-to-all-start.2 = ((f32[2,16,16,64,128]{4,3,2,1,0:T(8,128)}), f32[2,16,16,64,128]{4,3,2,1,0:T(8,128)}, u32[]{:S(2)}, u32[]{:S(2)}) async-start(f32[2,16,16,64,128]{4,3,2,1,0:T(8,128)} %broadcast_select_fusion), calls=%async_computation.2 | async-start | bytes 33554432 | tf_op jit(solution)/shard_map/all_to_all | solution.py:82
  55.4 132.6 %all-gather.5.cloned.1.call-start = ((), (), s32[]{:S(2)}) async-start(), calls=%async_computation.5 | async-start | bytes 1769472 | tf_op jit(solution)/shard_map/all_gather | solution.py:111
  55.5 25.7 %copy-start.15 = (f32[4,128]{1,0:T(4,128)S(1)}, f32[4,128]{1,0:T(4,128)}, u32[]{:S(2)}) copy-start(f32[4,128]{1,0:T(4,128)} %param.32) | copy-start | bytes 6148
  112.0 12.3 %copy-start.17 = (bf16[1,768,4096]{2,1,0:T(8,128)(2,1)S(1)}, bf16[1,768,4096]{2,1,0:T(8,128)(2,1)}, u32[]{:S(2)}) copy-start(bf16[1,768,4096]{2,1,0:T(8,128)(2,1)} %all-gather.3.cloned.1.call-done) | copy-start | bytes 18874372
  124.3 9.1 %copy-start.18 = (bf16[4096,16]{0,1:T(8,128)(2,1)S(1)}, bf16[4096,16]{0,1:T(8,128)(2,1)}, u32[]{:S(2)}) copy-start(bf16[4096,16]{0,1:T(8,128)(2,1)} %param.30) | copy-start | bytes 393220
  137.7 3.8 copy-start.2
  141.5 3.1 copy-start.11
  143.1 11.5 %copy-start.3 = (bf16[16,48,1024]{2,0,1:T(8,128)(2,1)}, bf16[16,48,1024]{2,0,1:T(8,128)(2,1)S(1)}, u32[]{:S(2)}) copy-start(bf16[16,48,1024]{2,0,1:T(8,128)(2,1)S(1)} %get-tuple-element.8) | copy-start | bytes 4718596
  144.3 359.5 %reduce-scatter.2.cloned.1.call-start = ((), (), s32[]{:S(2)}) async-start(), calls=%async_computation.6 | async-start | bytes 14155776 | tf_op jit(solution)/shard_map/reduce_scatter | solution.py:145
  154.6 8.1 %copy-start.16 = (f32[16]{0:T(128)S(1)}, f32[16]{0:T(128)}, u32[]{:S(2)}) copy-start(f32[16]{0:T(128)} %param.33) | copy-start | bytes 196
  162.6 6.1 %copy-start.5 = (bf16[16,48,1024]{2,0,1:T(8,128)(2,1)S(1)}, bf16[16,48,1024]{2,0,1:T(8,128)(2,1)}, u32[]{:S(2)}) copy-start(bf16[16,48,1024]{2,0,1:T(8,128)(2,1)} %get-tuple-element.10) | copy-start | bytes 4718596
  165.0 6.4 %copy-start.6 = (f32[16,48,16]{2,0,1:T(8,128)}, f32[16,48,16]{2,0,1:T(8,128)S(1)}, u32[]{:S(2)}) copy-start(f32[16,48,16]{2,0,1:T(8,128)S(1)} %fusion.32) | copy-start | bytes 147460
  216.4 3.6 copy-start.8
  216.4 3.6 copy-start.9
  216.4 3.6 copy-start.10
  216.4 3.6 copy-start.20
  299.0 0.7 copy-start.13
  299.0 1.0 copy-start.7
  299.0 1.5 copy-start.4
  307.1 199.0 %copy-start.1 = (bf16[4096,128]{1,0:T(8,128)(2,1)S(1)}, bf16[4096,128]{1,0:T(8,128)(2,1)}, u32[]{:S(2)}) copy-start(bf16[4096,128]{1,0:T(8,128)(2,1)} %param.29) | copy-start | bytes 3145732
Sparse Core Ops, SparseCore 0:
  10.2 101.7 all-gather.2
  144.5 43.4 all-gather.4
  299.1 204.6 reduce-scatter.1
where the time goes:
time: 519 us; the launch traced here: 513 us
  waiting for transfers between devices  236 us (45%)
  matrix products  86.9 us (17%)
  local copies, waits for them, and re-layouts  71.5 us (14%)
  other arithmetic  52.4 us (10%)
  blocking collectives  34.6 us (7%)
  starting transfers between devices  16.7 us (3%)
  between operations  14.6 us (3%)
    reduce_scatter x1, waiting for transfers between devices, local(): lax.psum_scatter(jnp.dot(normed, w_out, preferred_element_type=jnp.float3...  181 us
    psum x1, blocking collectives, local(): group_total = lax.psum(group_part, 'tensor')  34.6 us
    all_gather x1, waiting for transfers between devices, local(): flat_rows = lax.all_gather(suffix_acts, 'tensor', axis=1, tiled=True)[0]  30.7 us
    dot_general x1, matrix products, scan_block(): jnp.einsum('...tsh,...shp->...thp', weights, values, precision=highest)  20.2 us
    dot_general x1, matrix products, scan_block(): jnp.einsum('...shp,...shn->...hpn', scaled_vals, b_rows, precision=highest)  16.1 us
    another operation x2, local copies, waits for them, and re-layouts, local(): projected = projected[0].reshape(requests, -1, projected.shape[-1])  13.8 us
    all_to_all x1, waiting for transfers between devices, local(): lax.all_to_all(send_state, 'dp', split_axis=0, concat_axis=0, tiled=True)  13.5 us
    select_n x1, other arithmetic, local(): jnp.where(from_me[:, :, None, None, None], cache_states[hit_slot], 0.0)  12.4 us
  transfers between devices with their start and end apart: 6, of which 4 were waited for; matrix products, arithmetic and copies ran while one was open for 19% of the time, Pallas kernels for 0%

commit v1 on v0

--- a/solution.py
+++ b/solution.py
@@ -1,6 +1,8 @@
 import jax
 import jax.numpy as jnp
 from jax import lax
+from jax.experimental import pallas as pl
+from jax.experimental.pallas import tpu as pltpu
 from jax.sharding import PartitionSpec as P
 
 HEADS = 128
@@ -50,7 +52,7 @@
     return (outputs, end_state)
 
 
-def local(
+def local_plain(
     suffix_acts,
     suffix_lens,
     hit_holder,
@@ -156,9 +158,293 @@
     )
 
 
+def scan_kernel(
+    slot_ref,
+    mine_ref,
+    len_ref,
+    raw_x_ref,
+    raw_z_ref,
+    dt_ref,
+    dt_t_ref,
+    bc_ref,
+    own_x_ref,
+    got_x_ref,
+    own_state_ref,
+    got_state_ref,
+    conv_ref,
+    bias_ref,
+    bias_t_ref,
+    decay_ref,
+    decay_t_ref,
+    skip_ref,
+    gated_ref,
+    part_ref,
+    state_ref,
+    tail_ref,
+    ext_ref,
+):
+    q = pl.program_id(0)
+    mine = mine_ref[q] == 1
+    length = len_ref[q]
+    seq, width = raw_x_ref.shape
+    heads = dt_ref.shape[-1]
+    pad = 8
+    tail = jnp.where(
+        mine, own_x_ref[0].astype(jnp.float32), got_x_ref[0].astype(jnp.float32)
+    )
+    ext_ref[0:pad, :] = jnp.zeros((pad, width), jnp.float32)
+    ext_ref[pl.ds(pad - KT, KT), :] = tail
+    ext_ref[pl.ds(pad, seq), :] = raw_x_ref[...].astype(jnp.float32)
+    picked = lax.broadcasted_iota(jnp.int32, (pad, pad + seq), 1) == (
+        lax.broadcasted_iota(jnp.int32, (pad, pad + seq), 0) + (pad - KT + length)
+    )
+    tail_ref[0] = jnp.dot(
+        picked.astype(jnp.bfloat16),
+        ext_ref[0 : pad + seq, :].astype(jnp.bfloat16),
+        preferred_element_type=jnp.float32,
+    )[:KT].astype(jnp.bfloat16)
+
+    step = jnp.where(
+        lax.broadcasted_iota(jnp.int32, (seq, heads), 0) < length,
+        jax.nn.softplus(dt_ref[0] + bias_ref[...]),
+        0.0,
+    )
+    step_t = jnp.where(
+        lax.broadcasted_iota(jnp.int32, (heads, seq), 1) < length,
+        jax.nn.softplus(dt_t_ref[0] + bias_t_ref[...]),
+        0.0,
+    )
+    rows = lax.broadcasted_iota(jnp.int32, (seq, seq), 0)
+    cols = lax.broadcasted_iota(jnp.int32, (seq, seq), 1)
+    causal = rows >= cols
+    log_sum = jnp.dot(
+        causal.astype(jnp.float32),
+        -decay_ref[...] * step,
+        precision=highest,
+        preferred_element_type=jnp.float32,
+    )
+    log_sum_t = jnp.dot(
+        -decay_t_ref[...] * step_t,
+        (rows <= cols).astype(jnp.float32),
+        precision=highest,
+        preferred_element_type=jnp.float32,
+    )
+    half = GROUPS * NSTATE
+    contract_last = (((1,), (1,)), ((), ()))
+    contract_first = (((0,), (0,)), ((), ()))
+    b_rows = [bc_ref[:, g * NSTATE : (g + 1) * NSTATE] for g in range(GROUPS)]
+    c_rows = [bc_ref[:, half + g * NSTATE : half + (g + 1) * NSTATE] for g in range(GROUPS)]
+    scores = [
+        lax.dot_general(
+            c_rows[g], b_rows[g], contract_last, preferred_element_type=jnp.float32
+        )
+        for g in range(GROUPS)
+    ]
+    c_pair = [jnp.concatenate([c_rows[g], c_rows[g + 1]], axis=0) for g in range(0, GROUPS, 2)]
+    b_pair = [jnp.concatenate([b_rows[g], b_rows[g + 1]], axis=1) for g in range(0, GROUPS, 2)]
+    lanes = 2 * HDIM
+    first = lax.broadcasted_iota(jnp.int32, (seq, lanes), 1) < HDIM
+    squares = [jnp.zeros((seq, lanes), jnp.float32) for _ in range(GROUPS // 2)]
+    for pair in range(heads // 2):
+        h = 2 * pair
+        g = h % GROUPS
+        span = slice(pair * lanes, (pair + 1) * lanes)
+        running = conv_ref[0:1, span] * ext_ref[pad - KT : pad - KT + seq, span]
+        for k in range(1, KT + 1):
+            running = running + (
+                conv_ref[k : k + 1, span] * ext_ref[pad - KT + k : pad - KT + k + seq, span]
+            )
+        act = (running / (1.0 + jnp.exp(-running))).astype(jnp.bfloat16)
+        values = act.astype(jnp.float32)
+        wide = [jnp.broadcast_to(log_sum[:, h + i : h + i + 1], (seq, lanes)) for i in range(2)]
+        mats = []
+        for i in range(2):
+            gap = jnp.minimum(wide[i][:, :seq] - log_sum_t[h + i : h + i + 1, :], 0.0)
+            decay = jnp.where(causal, jnp.exp(gap), 0.0)
+            mats.append(
+                (scores[g + i] * decay * step_t[h + i : h + i + 1, :]).astype(jnp.bfloat16)
+            )
+        inner = jnp.dot(
+            jnp.concatenate(mats, axis=0), act, preferred_element_type=jnp.float32
+        )
+        start = jnp.where(
+            mine,
+            own_state_ref[0, h : h + 2],
+            got_state_ref[0, h : h + 2].astype(jnp.float32),
+        ).reshape(lanes, NSTATE)
+        carried = lax.dot_general(
+            c_pair[g // 2],
+            start.astype(jnp.bfloat16),
+            contract_last,
+            preferred_element_type=jnp.float32,
+        )
+        log_pair = jnp.where(first, wide[0], wide[1])
+        step_pair = jnp.where(first, step[:, h : h + 1], step[:, h + 1 : h + 2])
+        out = jnp.where(first, inner[:seq], inner[seq:]) + jnp.exp(log_pair) * jnp.where(
+            first, carried[:seq], carried[seq:]
+        )
+        out = out + skip_ref[:, span] * values
+        z = raw_z_ref[:, span].astype(jnp.float32)
+        gated = out * (z / (1.0 + jnp.exp(-z)))
+        gated_ref[:, span] = gated
+        squares[g // 2] = squares[g // 2] + gated * gated
+        last = log_pair[seq - 1 : seq, :]
+        scaled = (jnp.exp(last - log_pair) * step_pair * values).astype(jnp.bfloat16)
+        added = lax.dot_general(
+            scaled, b_pair[g // 2], contract_first, preferred_element_type=jnp.float32
+        )
+        for i in range(2):
+            fade = jnp.exp(wide[i][seq - 1 : seq, :])
+            state_ref[0, h + i] = (
+                fade * start[i * HDIM : (i + 1) * HDIM]
+                + added[i * HDIM : (i + 1) * HDIM, i * NSTATE : (i + 1) * NSTATE]
+            )
+    total = []
+    for value in squares:
+        total.append(jnp.sum(jnp.where(first, value, 0.0), axis=1, keepdims=True))
+        total.append(jnp.sum(jnp.where(first, 0.0, value), axis=1, keepdims=True))
+    part_ref[...] = jnp.concatenate(total, axis=1)
+
+
+def scan_call(
+    slot, mine, lengths, raw_x, raw_z, dt, dt_t, every_bc, own_x, got_x, own_state, got_state,
+    conv_x, dt_bias, decay_rate, skip_gain,
+):
+    requests = lengths.shape[0]
+    heads = dt.shape[-1]
+    seq = dt.shape[1]
+    width = raw_x.shape[1]
+    whole = lambda *shape: pl.BlockSpec(shape, lambda q, *_: (0,) * len(shape))
+    row = lambda n: pl.BlockSpec((seq, n), lambda q, *_: (q, 0))
+    by_q = lambda *shape: pl.BlockSpec((1, *shape), lambda q, *_: (q,) + (0,) * len(shape))
+    by_slot = lambda *shape: pl.BlockSpec(
+        (1, *shape), lambda q, slots, *_: (slots[q],) + (0,) * len(shape)
+    )
+    return pl.pallas_call(
+        scan_kernel,
+        grid_spec=pltpu.PrefetchScalarGridSpec(
+            num_scalar_prefetch=3,
+            grid=(requests,),
+            in_specs=[
+                row(width),
+                row(width),
+                by_q(seq, heads),
+                by_q(heads, seq),
+                row(every_bc.shape[1]),
+                by_slot(KT, width),
+                by_q(KT, width),
+                by_slot(heads, HDIM, NSTATE),
+                by_q(heads, HDIM, NSTATE),
+                whole(*conv_x.shape),
+                whole(1, heads),
+                whole(heads, 1),
+                whole(1, heads),
+                whole(heads, 1),
+                whole(1, width),
+            ],
+            out_specs=[
+                row(width),
+                row(GROUPS),
+                by_q(heads, HDIM, NSTATE),
+                by_q(KT, width),
+            ],
+            scratch_shapes=[pltpu.VMEM((seq + 16, width), jnp.float32)],
+        ),
+        out_shape=[
+            jax.ShapeDtypeStruct((requests * seq, width), jnp.float32),
+            jax.ShapeDtypeStruct((requests * seq, GROUPS), jnp.float32),
+            jax.ShapeDtypeStruct((requests, heads, HDIM, NSTATE), jnp.float32),
+            jax.ShapeDtypeStruct((requests, KT, width), jnp.bfloat16),
+        ],
+        compiler_params=pltpu.CompilerParams(vmem_limit_bytes=32 * 1024 * 1024),
+        cost_estimate=pl.CostEstimate(
+            flops=2 * requests * heads * seq * (seq * HDIM + 2 * HDIM * NSTATE),
+            bytes_accessed=requests * heads * HDIM * NSTATE * 10,
+            transcendentals=requests * seq * width * 4,
+        ),
+        name="scan",
+    )(
+        slot, mine, lengths, raw_x, raw_z, dt, dt_t, every_bc, own_x, got_x, own_state, got_state,
+        conv_x, dt_bias[None], dt_bias[:, None], decay_rate[None], decay_rate[:, None],
+        jnp.repeat(skip_gain, HDIM)[None],
+    )
+
+
+def local(
+    suffix_acts,
+    suffix_lens,
+    hit_holder,
+    hit_slot,
+    cache_states,
+    cache_conv_x,
+    cache_conv_bc,
+    w_in_x,
+    w_in_z,
+    w_in_bc,
+    w_in_dt,
+    conv_x,
+    conv_bc,
+    dt_bias,
+    decay_rate,
+    skip_gain,
+    norm_gain,
+    w_out,
+):
+    replica = lax.axis_index("dp")
+    lengths = suffix_lens[0]
+    requests = lengths.shape[0]
+    slot = jnp.where(replica == 0, hit_slot[0], hit_slot[1])
+    other_slot = jnp.where(replica == 0, hit_slot[1], hit_slot[0])
+    mine = jnp.where(replica == 0, hit_holder[0], hit_holder[1]) == replica
+    swap = [(0, 1), (1, 0)]
+    got_bc = lax.ppermute(cache_conv_bc[other_slot], "dp", swap)
+    got_x = lax.ppermute(cache_conv_x[other_slot], "dp", swap)
+    got_state = lax.ppermute(cache_states[other_slot].astype(jnp.bfloat16), "dp", swap)
+    tail_bc = jnp.where(mine[:, None, None], cache_conv_bc[slot], got_bc)
+    local_x = w_in_x.shape[1]
+    local_bc = w_in_bc.shape[1]
+    local_heads = w_in_dt.shape[1]
+    flat_rows = lax.all_gather(suffix_acts, "tensor", axis=1, tiled=True)[0]
+    seq_len = flat_rows.shape[0] // requests
+    raw_bc = jnp.dot(flat_rows, w_in_bc, preferred_element_type=jnp.float32)
+    raw_bc = raw_bc.astype(jnp.bfloat16).reshape(requests, seq_len, local_bc)
+    ext_bc, act_bc = causal_conv(tail_bc, raw_bc, conv_bc)
+    every_bc = lax.all_gather(
+        act_bc.reshape(requests * seq_len, local_bc), "tensor", axis=1, tiled=True
+    )
+    raw_x = jnp.dot(flat_rows, w_in_x, preferred_element_type=jnp.float32).astype(jnp.bfloat16)
+    raw_z = jnp.dot(flat_rows, w_in_z, preferred_element_type=jnp.float32).astype(jnp.bfloat16)
+    raw_dt = jnp.dot(flat_rows, w_in_dt, preferred_element_type=jnp.float32)
+    dt = raw_dt.reshape(requests, seq_len, local_heads)
+    new_tail_bc = last_rows(ext_bc, lengths)
+    gated, part, new_states, new_tail_x = scan_call(
+        slot, mine.astype(jnp.int32), lengths, raw_x, raw_z, dt, dt.transpose(0, 2, 1), every_bc,
+        cache_conv_x, got_x, cache_states, got_state, conv_x, dt_bias, decay_rate, skip_gain,
+    )
+    total = lax.psum(part, "tensor")
+    inverse = lax.rsqrt(total / (HEADS // GROUPS * HDIM) + epsilon)
+    live = jnp.arange(seq_len, dtype=jnp.int32)[None, :] < lengths[:, None]
+    inverse = jnp.where(live.reshape(-1)[:, None], inverse, 0.0)
+    inverse = jnp.repeat(jnp.tile(inverse, (1, local_heads // GROUPS)), HDIM, axis=1)
+    normed = (gated * inverse * norm_gain).astype(jnp.bfloat16)
+    mixed_out = lax.psum_scatter(
+        jnp.dot(normed, w_out, preferred_element_type=jnp.float32).astype(jnp.bfloat16),
+        "tensor",
+        scatter_dimension=0,
+        tiled=True,
+    )
+    return (
+        mixed_out[None],
+        new_states[None],
+        new_tail_x[None],
+        new_tail_bc[None],
+    )
+
+
 def solution(mesh):
+    regular = mesh.shape["tensor"] == 8
     return jax.shard_map(
-        local,
+        local if regular else local_plain,
         mesh=mesh,
         in_specs=(
             P(("groups", "dp"), "tensor", None),

time: 519 us -> 371 us (0.71)
  other arithmetic: 52.4 us -> 1.56 us
  local copies, waits for them, and re-layouts: 71.5 us -> 27.5 us
  matrix products: 86.9 us -> 43.9 us
  Pallas kernels: 0 us -> 20.1 us
  starting transfers between devices: 16.7 us -> 1.2 us
  waiting for transfers between devices: 236 us -> 223 us
    reduce_scatter x1, waiting for transfers between devices: 181 us -> 114 us  [local(): lax.psum_scatter(jnp.dot(normed, w_out, preferred_element_type=jnp.float3...]
    all_gather x1, waiting for transfers between devices: 30.7 us -> 91.3 us  [local(): flat_rows = lax.all_gather(suffix_acts, 'tensor', axis=1, tiled=True)[0]]
    dot_general x6 -> x2, matrix products: 53.1 us -> 7.67 us  [the longest x1 4.59 us: local(): raw_bc = jnp.dot(flat_rows, w_in_bc, preferred_element_type=jnp.float32)]
    select_n x8 -> x3, other arithmetic: 21.2 us -> 1 us  [the longest x2 0.84 us: local(): tail_bc = jnp.where(mine[:, None, None], cache_conv_bc[slot], got_bc)]
    pallas_call x0 -> x1, Pallas kernels: none -> 20.1 us  [scan_call(): pl.pallas_call(scan_kernel, grid_spec=pltpu.PrefetchScalarGridSpec(num_sc...]
    all_to_all x3 -> x0, starting transfers between devices: 16.4 us -> none  [the longest x1 9.69 us: local(): lax.all_to_all(send_state, 'dp', split_axis=0, concat_axis=0, tiled=True)]
    another operation x3, local copies, waits for them, and re-layouts: 14.6 us -> 0.11 us  [the longest x1 0.08 us: scan_call(): jnp.repeat(skip_gain, HDIM)[None]]
    gather x6 -> x5, local copies, waits for them, and re-layouts: 24.1 us -> 10.1 us  [the longest x1 6.34 us: local(): cache_states[other_slot].astype(jnp.bfloat16)]
  transfers between devices with their start and end apart: 6 -> 6, of which waited for: 4 -> 3; matrix products, arithmetic and copies ran while one was open for 19% -> 13% of each run, Pallas kernels for 0% -> 0%
where the time goes in v1:
time: 371 us; the launch traced here: 370 us
  waiting for transfers between devices  223 us (60%)
  matrix products  43.9 us (12%)
  blocking collectives  38.8 us (10%)
  local copies, waits for them, and re-layouts  27.5 us (7%)
  Pallas kernels  20.1 us (5%)
  between operations  14.1 us (4%)
    reduce_scatter x1, waiting for transfers between devices, local(): lax.psum_scatter(jnp.dot(normed, w_out, preferred_element_type=jnp.float3...  114 us
    all_gather x1, waiting for transfers between devices, local(): flat_rows = lax.all_gather(suffix_acts, 'tensor', axis=1, tiled=True)[0]  91.3 us
    psum x1, blocking collectives, local(): total = lax.psum(part, 'tensor')  38.8 us
    pallas_call x1, Pallas kernels, scan_call(): pl.pallas_call(scan_kernel, grid_spec=pltpu.PrefetchScalarGridSpec(num_sc...  20.1 us
    all_gather x1, waiting for transfers between devices, local(): lax.all_gather(act_bc.reshape(requests * seq_len, local_bc), 'tensor', ax...  16.9 us
    dot_general x1, matrix products, local(): jnp.dot(normed, w_out, preferred_element_type=jnp.float32)  13 us
    dot_general x1, matrix products, local(): jnp.dot(flat_rows, w_in_x, preferred_element_type=jnp.float32)  12.2 us
    dot_general x1, matrix products, local(): jnp.dot(flat_rows, w_in_z, preferred_element_type=jnp.float32)  11.1 us
  transfers between devices with their start and end apart: 6, of which 3 were waited for; matrix products, arithmetic and copies ran while one was open for 13% of the time, Pallas kernels for 0%

profile of v1, /device:TPU:0, one launch (start us, length us, event | category | flops | bytes accessed | tf_op | source)
XLA Modules:
  0.0 370.1 jit_solution(9254420871262035800)
XLA Ops:
  7.2 0.0 copy-start
  7.2 0.0 copy-start.11
  7.2 0.0 copy-start.10
  7.2 0.0 copy-start.14
  7.2 0.0 copy-start.6
  7.2 0.0 copy-start.13
  7.3 0.0 all-gather.3.cloned.1.call-start
  7.3 0.7 all-gather.3.cloned.1.call-update
  8.0 0.0 all-gather.5.cloned.1.call-start
  8.1 0.8 fusion.28
  8.8 1.3 gather_fusion.1
  10.1 0.5 collective-permute-start
  10.7 1.7 gather_fusion.2
  12.4 0.1 copy.34
  12.5 0.1 collective-permute-start.1
  12.6 6.3 %gather_fusion.3 = bf16[16,16,64,128]{3,2,1,0:T(8,128)(2,1)} fusion(f32[16,16,64,128]{3,2,1,0:T(8,128)} %own_state_ref.1, s32[1024]{0:T(1024)S(1)} %pad_clamp_fusion), kind=kCustom, calls=%fused_computation.3 | custom fusion | bytes 8388672 | tf_op jit(solution)/shard_map/gather | solution.py:402
  19.0 0.5 collective-permute-start.2
  19.4 0.1 iota_compare_fusion
  19.5 0.1 copy.36.own_x_ref
  19.6 0.1 lt.63
  19.7 0.6 gather_fusion
  20.3 0.1 broadcast_in_dim.70
  20.4 0.1 broadcast_in_dim_reshape.4.skip_ref
  20.5 0.1 copy.38.decay_t_ref
  20.6 0.1 copy.37.bias_t_ref
  20.7 0.0 collective-permute-done
  20.7 0.1 broadcast_select_fusion.1
  20.8 91.3 %all-gather.3.cloned.1.call-done = bf16[1,768,4096]{2,1,0:T(8,128)(2,1)} async-done(((bf16[1,96,4096]{2,1,0:T(8,128)(2,1)}), bf16[1,768,4096]{2,1,0:T(8,128)(2,1)}) %all-gather.3.cloned.1.call-update) | async-done | bytes 6291472 | tf_op jit(solution)/shard_map/all_gather | solution.py:407
  112.0 4.6 %fusion.13 = bf16[768,128]{1,0:T(8,128)(2,1)S(1)} fusion(bf16[4096,128]{1,0:T(8,128)(2,1)S(1)} %copy-done, bf16[1,768,4096]{2,1,0:T(8,128)(2,1)} %all-gather.3.cloned.1.call-done), kind=kOutput, calls=%fused_computation.16 | convolution fusion | flops 805404672 | bytes 7536640 | tf_op jit(solution)/shard_map/dot_general | solution.py:409
  116.6 0.1 copy.31
  116.7 0.2 multiply_convert_fusion.2
  116.9 0.7 copy.33
  117.6 0.0 all-gather.5.cloned.1.call-update
  117.7 0.0 reduce-scatter.2.cloned.1.call-start
  117.7 0.0 slice-start
  117.7 11.1 %fusion.9.raw_z_ref = bf16[768,1024]{1,0:T(8,128)(2,1)S(1)} fusion(bf16[4096,1024]{1,0:T(8,128)(2,1)} %param.26, bf16[1,768,4096]{2,1,0:T(8,128)(2,1)} %all-gather.3.cloned.1.call-done), kind=kOutput, calls=%fused_computation.14 | convolution fusion | flops 6443237376 | bytes 16252928 | tf_op jit(solution)/shard_map/dot_general | solution.py:416
  128.8 0.0 slice-start.1
  128.8 0.0 copy-start.12
  128.8 12.2 %fusion.6.raw_x_ref = bf16[768,1024]{1,0:T(8,128)(2,1)} fusion(bf16[4096,1024]{1,0:T(8,128)(2,1)} %param.25, bf16[1,768,4096]{2,1,0:T(8,128)(2,1)} %all-gather.3.cloned.1.call-done), kind=kOutput, calls=%fused_computation.13 | convolution fusion | flops 6443237376 | bytes 16252928 | tf_op jit(solution)/shard_map/dot_general | solution.py:415
  141.1 3.1 fusion.19
  144.1 0.2 copy.35.dt_ref
  144.3 0.0 collective-permute-done.1.got_x_ref
  144.3 0.0 collective-permute-done.2.got_state_ref
  144.3 16.9 %all-gather.5.cloned.1.call-done.bc_ref = bf16[768,1024]{1,0:T(8,128)(2,1)} async-done(((bf16[768,128]{1,0:T(8,128)(2,1)}), bf16[768,1024]{1,0:T(8,128)(2,1)}) %all-gather.5.cloned.1.call-update) | async-done | bytes 1572880 | tf_op jit(solution)/shard_map/all_gather | solution.py:412
  161.2 3.4 copy-done.2
  164.6 1.4 copy-done.3
  166.0 1.4 copy-done.4
  167.4 20.1 %scan.1 = (f32[768,1024]{1,0:T(8,128)S(1)}, f32[768,4]{1,0:T(8,128)S(1)}, f32[16,16,64,128]{3,2,1,0:T(8,128)}, bf16[16,3,1024]{2,1,0:T(4,128)(2,1)S(1)}) custom-call(s32[16]{0:T(128)S(1)} %bitcast.72, s32[16]{0:T(128)S(1)} %get-tuple-element.22.mine_ref, s32[16]{0:T(128)S(1)} %bitcast.65, bf16[768,1024]{1,0:T(8,128)(2,1)S(1)} %copy-done.4, ...), custom_call_target="tpu_custom_call" | custom-call | flops 478150656 | bytes 20971520 | tf_op jit(solution)/shard_map/scan/pallas_call | solution.py:323
  187.5 1.7 copy-done.9
  189.3 38.8 %psum.7 = f32[768,4]{1,0:T(8,128)S(1)} all-reduce(f32[768,4]{1,0:T(8,128)S(1)} %get-tuple-element.9), channel_id=1, replica_groups=mesh['groups'=2,'dp'=2,'tensor'=8] {'tensor'}, use_global_device_ids=true, to_apply=%region_0.1 | all-reduce | flops 3072 | bytes 24576 | tf_op jit(solution)/shard_map/psum | solution.py:424
  228.1 0.2 rsqrt_select_fusion
  228.3 0.1 copy.39
  228.4 1.9 broadcast_in_dim.73
  230.3 3.6 copy.40
  233.9 13.0 %convolution_convert_fusion = bf16[768,4096]{1,0:T(8,128)(2,1)} fusion(bf16[1024,4096]{1,0:T(8,128)(2,1)} %param.35, f32[768,1024]{1,0:T(8,128)} %copy-done.9, f32[768,1024]{1,0:T(8,128)} %copy.40, f32[1024]{0:T(1024)S(1)} %copy-done.16), kind=kOutput, calls=%fused_computation.5 | convolution fusion | flops 6447955968 | bytes 20975616 | tf_op jit(solution)/shard_map/dot_general | solution.py:431
  246.9 0.0 reduce-scatter.2.cloned.1.call-update
  246.9 0.1 fusion.23
  247.0 0.1 reshape.222
  247.1 0.1 fusion.26
  247.2 1.0 gather_fusion.4
  248.2 0.1 broadcast_select_fusion
  248.3 0.6 copy.42
  248.9 0.7 copy.41
  249.6 113.9 %reduce-scatter.2.cloned.1.call-done = bf16[96,4096]{1,0:T(8,128)(2,1)} async-done(((bf16[768,4096]{1,0:T(8,128)(2,1)}), bf16[96,4096]{1,0:T(8,128)(2,1)}) %reduce-scatter.2.cloned.1.call-update) | async-done | bytes 786448 | tf_op jit(solution)/shard_map/reduce_scatter | solution.py:430
  (34 shorter events, 0.1 us)
Async XLA Ops:
  7.2 104.9 %copy-start = (bf16[4096,128]{1,0:T(8,128)(2,1)S(1)}, bf16[4096,128]{1,0:T(8,128)(2,1)}, u32[]{:S(2)}) copy-start(bf16[4096,128]{1,0:T(8,128)(2,1)} %param.27) | copy-start | bytes 3145732
  7.2 12.5 %copy-start.11 = (bf16[16,3,128]{2,0,1:T(8,128)(2,1)S(1)}, bf16[16,3,128]{2,0,1:T(8,128)(2,1)}, u32[]{:S(2)}) copy-start(bf16[16,3,128]{2,0,1:T(8,128)(2,1)} %param.24) | copy-start | bytes 36868
  7.2 12.3 %copy-start.10 = (bf16[16,3,1024]{2,0,1:T(8,128)(2,1)S(1)}, bf16[16,3,1024]{2,0,1:T(8,128)(2,1)}, u32[]{:S(2)}) copy-start(bf16[16,3,1024]{2,0,1:T(8,128)(2,1)} %param.23) | copy-start | bytes 294916
  7.2 12.2 %copy-start.14 = (s32[2,16]{1,0:T(2,128)S(1)}, s32[2,16]{1,0:T(2,128)}, u32[]{:S(2)}) copy-start(s32[2,16]{1,0:T(2,128)} %param.20) | copy-start | bytes 388
  7.2 12.2 %copy-start.6 = (s32[1,16]{1,0:T(1,128)S(1)}, s32[1,16]{1,0:T(1,128)}, u32[]{:S(2)}) copy-start(s32[1,16]{1,0:T(1,128)} %param.19) | copy-start | bytes 196
  7.2 12.3 %copy-start.13 = (f32[4,128]{1,0:T(4,128)S(1)}, f32[4,128]{1,0:T(4,128)}, u32[]{:S(2)}) copy-start(f32[4,128]{1,0:T(4,128)} %param.30) | copy-start | bytes 6148
  7.2 13.1 %copy-start.15 = (f32[16]{0:T(128)S(1)}, f32[16]{0:T(128)}, u32[]{:S(2)}) copy-start(f32[16]{0:T(128)} %param.33) | copy-start | bytes 196
  7.2 13.3 %copy-start.8 = (f32[16]{0:T(128)S(1)}, f32[16]{0:T(128)}, u32[]{:S(2)}) copy-start(f32[16]{0:T(128)} %param.32) | copy-start | bytes 196
  7.3 13.3 %copy-start.7 = (f32[16]{0:T(128)S(1)}, f32[16]{0:T(128)}, u32[]{:S(2)}) copy-start(f32[16]{0:T(128)} %param.31) | copy-start | bytes 196
  7.3 104.8 %all-gather.3.cloned.1.call-start = ((), (), s32[]{:S(2)}) async-start(), calls=%async_computation.1 | async-start | bytes 7077888 | tf_op jit(solution)/shard_map/all_gather | solution.py:407
  8.0 153.2 %all-gather.5.cloned.1.call-start = ((), (), s32[]{:S(2)}) async-start(), calls=%async_computation.2 | async-start | bytes 1769472 | tf_op jit(solution)/shard_map/all_gather | solution.py:412
  10.1 10.5 %collective-permute-start = (bf16[16,3,128]{2,0,1:T(8,128)(2,1)S(1)}, bf16[16,3,128]{2,0,1:T(8,128)(2,1)S(1)}, u32[]{:S(2)}, u32[]{:S(2)}) collective-permute-start(bf16[16,3,128]{2,0,1:T(8,128)(2,1)S(1)} %gather_fusion.1), channel_id=1, source_target_pairs={{0,8},{8,0},{1,9},{9,1},{2,10},{10,2},{3,11},{11,3},{4,12},{12,4},... | collective-permute-start | bytes 36872 | tf_op jit(solution)/shard_map/ppermute | solution.py:400
  12.5 131.8 %collective-permute-start.1 = (bf16[16,3,1024]{2,1,0:T(4,128)(2,1)S(1)}, bf16[16,3,1024]{2,1,0:T(4,128)(2,1)S(1)}, u32[]{:S(2)}, u32[]{:S(2)}) collective-permute-start(bf16[16,3,1024]{2,1,0:T(4,128)(2,1)S(1)} %copy.34), channel_id=1, source_target_pairs={{0,8},{8,0},{1,9},{9,1},{2,10},{10,2},{3,11},{11,3},{4,12},{12,4},... | collective-permute-start | bytes 294920 | tf_op jit(solution)/shard_map/ppermute | solution.py:401
  19.0 125.4 %collective-permute-start.2 = (bf16[16,16,64,128]{3,2,1,0:T(8,128)(2,1)}, bf16[16,16,64,128]{3,2,1,0:T(8,128)(2,1)}, u32[]{:S(2)}, u32[]{:S(2)}) collective-permute-start(bf16[16,16,64,128]{3,2,1,0:T(8,128)(2,1)} %gather_fusion.3), channel_id=1, source_target_pairs={{0,8},{8,0},{1,9},{9,1},{2,10},{10,2},{3,11},{11,3},{4,12},{12,4},... | collective-permute-start | bytes 12582920 | tf_op jit(solution)/shard_map/ppermute | solution.py:402
  117.7 245.9 %reduce-scatter.2.cloned.1.call-start = ((), (), s32[]{:S(2)}) async-start(), calls=%async_computation.3 | async-start | bytes 7077888 | tf_op jit(solution)/shard_map/reduce_scatter | solution.py:430
  117.7 23.3 %slice-start = ((s8[6291456]{0:T(1024)(128)(4,1)}), s8[4194304]{0:T(1024)(128)(4,1)S(1)}, s32[]{:S(2)}) async-start(s8[6291456]{0:T(1024)(128)(4,1)} %bitcast.74), calls=%async_computation.4 | async-start | bytes 8388608
  128.8 12.3 %slice-start.1 = ((s8[6291456]{0:T(1024)(128)(4,1)}), s8[2097152]{0:T(1024)(128)(4,1)S(1)}, s32[]{:S(2)}) async-start(s8[6291456]{0:T(1024)(128)(4,1)} %bitcast.74), calls=%async_computation.5 | async-start | bytes 4194304
  128.8 12.3 %copy-start.12 = (bf16[4096,16]{0,1:T(8,128)(2,1)S(1)}, bf16[4096,16]{0,1:T(8,128)(2,1)}, u32[]{:S(2)}) copy-start(bf16[4096,16]{0,1:T(8,128)(2,1)} %param.28) | copy-start | bytes 393220
  141.0 20.2 %copy-start.5 = (f32[4,1024]{1,0:T(4,128)S(1)}, f32[4,1024]{1,0:T(4,128)}, u32[]{:S(2)}) copy-start(f32[4,1024]{1,0:T(4,128)} %conv_ref.1) | copy-start | bytes 49156
  161.2 3.4 copy-start.2
  164.6 1.4 copy-start.3
  166.0 1.4 copy-start.4
  187.5 1.7 copy-start.9
  189.3 44.6 %copy-start.16 = (f32[1024]{0:T(1024)S(1)}, f32[1024]{0:T(1024)}, u32[]{:S(2)}) copy-start(f32[1024]{0:T(1024)} %param.34) | copy-start | bytes 12292
  233.9 129.6 %copy-start.1 = (bf16[4096,128]{1,0:T(8,128)(2,1)S(1)}, bf16[4096,128]{1,0:T(8,128)(2,1)}, u32[]{:S(2)}) copy-start(bf16[4096,128]{1,0:T(8,128)(2,1)} %param.27) | copy-start | bytes 3145732
Sparse Core Ops, SparseCore 0:
  10.3 101.7 all-gather.2
  117.8 43.3 all-gather.4
  247.0 116.4 reduce-scatter.1

commit v2 on v1

--- a/solution.py
+++ b/solution.py
@@ -156,6 +156,348 @@
         new_tail_x[None],
         new_tail_bc[None],
     )
+
+
+LINE = 4
+
+
+def place():
+    me = lax.axis_index("tensor")
+    return me, me // 2, me % 2
+
+
+def nearest(z, k):
+    low = z < 2
+    near = jnp.where(low, z, LINE - 1 - z)
+    pick = jnp.where(near == 0, k, (1, 0, 2, 3)[k])
+    return jnp.where(low, pick, LINE - 1 - pick)
+
+
+def signal(device):
+    pl.semaphore_signal(
+        pltpu.get_barrier_semaphore(),
+        inc=1,
+        device_id={"tensor": device},
+        device_id_type=pl.DeviceIdType.MESH,
+    )
+
+
+def remote(source, target, send_sem, recv_sem, device):
+    return pltpu.make_async_remote_copy(
+        src_ref=source,
+        dst_ref=target,
+        send_sem=send_sem,
+        recv_sem=recv_sem,
+        device_id={"tensor": device},
+        device_id_type=pl.DeviceIdType.MESH,
+    )
+
+
+def project_kernel(
+    acts_ref, w_x_ref, w_bc_ref, w_dt_ref, rows_ref, x_ref, bc_ref, dt_ref,
+    held, x_buf, bc_buf, dt_buf, load_sem, store_sem, line_send, line_recv, side_send, side_recv,
+):
+    me, z, y = place()
+    part = acts_ref.shape[0]
+    side = me + 1 - 2 * y
+    loads = [
+        pltpu.make_async_copy(acts_ref, held.at[pl.ds(me * part, part)], load_sem.at[0]),
+        pltpu.make_async_copy(w_x_ref, x_buf, load_sem.at[1]),
+        pltpu.make_async_copy(w_bc_ref, bc_buf, load_sem.at[2]),
+        pltpu.make_async_copy(w_dt_ref, dt_buf, load_sem.at[3]),
+    ]
+    for load in loads:
+        load.start()
+    signal(side)
+
+    @pl.when(z < LINE - 1)
+    def _():
+        signal(me + 2)
+
+    @pl.when(z > 0)
+    def _():
+        signal(me - 2)
+
+    ends = (z == 0) | (z == LINE - 1)
+    pl.semaphore_wait(pltpu.get_barrier_semaphore(), jnp.where(ends, 2, 3))
+
+    def spot(plane, column):
+        return held.at[pl.ds((2 * plane + column) * part, part)]
+
+    def up(plane):
+        return remote(
+            spot(plane, y), spot(plane, y), line_send.at[0, plane], line_recv.at[plane], me + 2
+        )
+
+    def down(plane):
+        return remote(
+            spot(plane, y), spot(plane, y), line_send.at[1, plane], line_recv.at[plane], me - 2
+        )
+
+    def across(plane):
+        return remote(
+            spot(plane, y), spot(plane, y), side_send.at[plane], side_recv.at[plane], side
+        )
+
+    def arrived(plane, column, sem):
+        return remote(spot(plane, column), spot(plane, column), line_send.at[0, 0], sem, side)
+
+    loads[0].wait()
+    for k in range(LINE + 1):
+        if k < LINE:
+            plane = nearest(z, k)
+            if k > 0:
+                arrived(plane, y, line_recv.at[plane]).wait_recv()
+
+            @pl.when((plane <= z) & (z < LINE - 1))
+            def _():
+                up(plane).start()
+
+            @pl.when((plane >= z) & (z > 0))
+            def _():
+                down(plane).start()
+
+            across(plane).start()
+        if k == 1:
+            for load in loads[1:]:
+                load.wait()
+        if k > 0:
+            plane = nearest(z, k - 1)
+            arrived(plane, 1 - y, side_recv.at[plane]).wait_recv()
+            span = pl.ds(plane * (2 * part), 2 * part)
+            pltpu.make_async_copy(held.at[span], rows_ref.at[span], store_sem.at[k - 1]).start()
+            bc_ref[span, :] = jnp.dot(
+                held[span, :], bc_buf[...], preferred_element_type=jnp.float32
+            ).astype(jnp.bfloat16)
+            dt_ref[span, :] = jnp.dot(
+                held[span, :], dt_buf[...], preferred_element_type=jnp.float32
+            )
+            tile = 256
+
+            def step(j, carry):
+                columns = pl.ds(pl.multiple_of(j * tile, tile), tile)
+                x_ref[span, columns] = jnp.dot(
+                    held[span, :], x_buf[:, columns], preferred_element_type=jnp.float32
+                ).astype(jnp.bfloat16)
+                return carry
+
+            lax.fori_loop(0, x_ref.shape[1] // tile, step, 0)
+    for k in range(LINE):
+        plane = nearest(z, k)
+
+        @pl.when((plane <= z) & (z < LINE - 1))
+        def _():
+            up(plane).wait_send()
+
+        @pl.when((plane >= z) & (z > 0))
+        def _():
+            down(plane).wait_send()
+
+        across(plane).wait_send()
+        span = pl.ds(plane * (2 * part), 2 * part)
+        pltpu.make_async_copy(held.at[span], rows_ref.at[span], store_sem.at[k]).wait()
+
+
+def project_call(acts, w_x, w_bc, w_dt):
+    part, depth = acts.shape
+    rows = part * 2 * LINE
+    vmem = pl.BlockSpec(memory_space=pltpu.VMEM)
+    hbm = pl.BlockSpec(memory_space=pl.ANY)
+    dma = pltpu.SemaphoreType.DMA
+    return pl.pallas_call(
+        project_kernel,
+        in_specs=[hbm] * 4,
+        out_specs=[hbm, vmem, vmem, vmem],
+        out_shape=[
+            jax.ShapeDtypeStruct((rows, depth), jnp.bfloat16),
+            jax.ShapeDtypeStruct((rows, w_x.shape[1]), jnp.bfloat16),
+            jax.ShapeDtypeStruct((rows, w_bc.shape[1]), jnp.bfloat16),
+            jax.ShapeDtypeStruct((rows, w_dt.shape[1]), jnp.float32),
+        ],
+        scratch_shapes=[
+            pltpu.VMEM((rows, depth), jnp.bfloat16),
+            pltpu.VMEM(w_x.shape, jnp.bfloat16),
+            pltpu.VMEM(w_bc.shape, jnp.bfloat16),
+            pltpu.VMEM(w_dt.shape, jnp.bfloat16),
+            dma((4,)),
+            dma((LINE,)),
+            dma((2, LINE)),
+            dma((LINE,)),
+            dma((LINE,)),
+            dma((LINE,)),
+        ],
+        compiler_params=pltpu.CompilerParams(
+            collective_id=0, has_side_effects=True, vmem_limit_bytes=40 * 1024 * 1024
+        ),
+        cost_estimate=pl.CostEstimate(
+            flops=2 * rows * depth * w_x.shape[1],
+            bytes_accessed=4 * rows * depth + 2 * depth * w_x.shape[1],
+            transcendentals=0,
+        ),
+        name="gather_project",
+    )(acts, w_x, w_bc, w_dt)
+
+
+def output_kernel(
+    gated_ref, part_ref, live_ref, member_ref, gain_ref, w_ref, out_ref,
+    parts, normed, w_buf, own, side_out, side_in, line_out, line_in,
+    load_sem, part_send, part_recv, side_send, side_recv, line_send, line_recv,
+):
+    me, z, y = place()
+    peers = 2 * LINE
+    rows, width = gated_ref.shape
+    chunk = rows // peers
+    side = me + 1 - 2 * y
+    load = pltpu.make_async_copy(w_ref, w_buf, load_sem)
+    load.start()
+    for hop in range(1, peers):
+        signal(lax.rem(me + hop, peers))
+    pl.semaphore_wait(pltpu.get_barrier_semaphore(), peers - 1)
+    sends = []
+    for hop in range(1, peers):
+        send = remote(
+            part_ref, parts.at[hop], part_send.at[hop], part_recv.at[hop], lax.rem(me + hop, peers)
+        )
+        send.start()
+        sends.append(send)
+    total = part_ref[...]
+    for hop in range(1, peers):
+        sends[hop - 1].wait_recv()
+        total = total + parts[hop]
+    inverse = lax.rsqrt(total / (HEADS // GROUPS * HDIM) + epsilon)
+    inverse = jnp.where(live_ref[...] > 0.0, inverse, 0.0)
+    high = inverse.astype(jnp.bfloat16)
+    low = (inverse - high.astype(jnp.float32)).astype(jnp.bfloat16)
+    both = jnp.concatenate([high, low], axis=0)
+    block = rows // 2
+    for i in range(2):
+        scale = lax.dot_general(
+            both[:, i * block : (i + 1) * block],
+            member_ref[...],
+            (((0,), (0,)), ((), ())),
+            preferred_element_type=jnp.float32,
+        )
+        span = slice(i * block, (i + 1) * block)
+        normed[span, :] = (gated_ref[span, :] * scale * gain_ref[...]).astype(jnp.bfloat16)
+    load.wait()
+
+    def across(plane):
+        return remote(
+            side_out.at[plane], side_in.at[plane], side_send.at[plane], side_recv.at[plane], side
+        )
+
+    def along(plane):
+        toward = jnp.where(plane > z, me + 2, me - 2)
+        slot = jnp.where((plane < z) & (plane == z - 1), LINE, plane)
+        return remote(
+            line_out.at[plane], line_in.at[slot], line_send.at[plane], line_recv.at[slot], toward
+        )
+
+    def line_arrived(slot):
+        return remote(line_in.at[slot], line_in.at[slot], line_send.at[0], line_recv.at[slot], side)
+
+    tile = 512
+    tiles = w_buf.shape[1] // tile
+    for k in range(LINE - 1, -1, -1):
+        plane = nearest(z, k)
+        span = pl.ds(plane * (2 * chunk), 2 * chunk)
+
+        def step(j, carry):
+            columns = pl.ds(pl.multiple_of(j * tile, tile), tile)
+            result = jnp.dot(
+                normed[span, :], w_buf[:, columns], preferred_element_type=jnp.float32
+            )
+            own[plane, :, columns] = jnp.where(y == 0, result[:chunk], result[chunk:])
+            side_out[plane, :, columns] = jnp.where(
+                y == 0, result[chunk:], result[:chunk]
+            ).astype(jnp.bfloat16)
+            return carry
+
+        lax.fori_loop(0, tiles, step, 0)
+        across(plane).start()
+    for k in range(LINE - 1, 0, -1):
+        plane = nearest(z, k)
+        across(plane).wait_recv()
+        joined = ((plane > z) & (z > 0)) | ((plane < z) & (z < LINE - 1))
+
+        @pl.when(joined)
+        def _():
+            line_arrived(plane).wait_recv()
+            line_out[plane] = (
+                own[plane]
+                + side_in[plane].astype(jnp.float32)
+                + line_in[plane].astype(jnp.float32)
+            ).astype(jnp.bfloat16)
+
+        @pl.when(jnp.logical_not(joined))
+        def _():
+            line_out[plane] = (own[plane] + side_in[plane].astype(jnp.float32)).astype(
+                jnp.bfloat16
+            )
+
+        along(plane).start()
+    across(z).wait_recv()
+    own[z] = own[z] + side_in[z].astype(jnp.float32)
+
+    @pl.when(z > 0)
+    def _():
+        line_arrived(z).wait_recv()
+        own[z] = own[z] + line_in[z].astype(jnp.float32)
+
+    @pl.when(z < LINE - 1)
+    def _():
+        line_arrived(LINE).wait_recv()
+        own[z] = own[z] + line_in[LINE].astype(jnp.float32)
+
+    out_ref[...] = own[z].astype(jnp.bfloat16)
+    for send in sends:
+        send.wait_send()
+    for k in range(LINE):
+        plane = nearest(z, k)
+        across(plane).wait_send()
+        if k > 0:
+            along(plane).wait_send()
+
+
+def output_call(gated, part, live, member, gain, w_out):
+    rows, width = gated.shape
+    depth = w_out.shape[1]
+    peers = 2 * LINE
+    chunk = rows // peers
+    vmem = pl.BlockSpec(memory_space=pltpu.VMEM)
+    dma = pltpu.SemaphoreType.DMA
+    return pl.pallas_call(
+        output_kernel,
+        in_specs=[vmem] * 5 + [pl.BlockSpec(memory_space=pl.ANY)],
+        out_specs=vmem,
+        out_shape=jax.ShapeDtypeStruct((chunk, depth), jnp.bfloat16),
+        scratch_shapes=[
+            pltpu.VMEM((peers, *part.shape), jnp.float32),
+            pltpu.VMEM((rows, width), jnp.bfloat16),
+            pltpu.VMEM(w_out.shape, jnp.bfloat16),
+            pltpu.VMEM((LINE, chunk, depth), jnp.float32),
+            pltpu.VMEM((LINE, chunk, depth), jnp.bfloat16),
+            pltpu.VMEM((LINE, chunk, depth), jnp.bfloat16),
+            pltpu.VMEM((LINE, chunk, depth), jnp.bfloat16),
+            pltpu.VMEM((LINE + 1, chunk, depth), jnp.bfloat16),
+            dma,
+            dma((peers,)),
+            dma((peers,)),
+            dma((LINE,)),
+            dma((LINE,)),
+            dma((LINE,)),
+            dma((LINE + 1,)),
+        ],
+        compiler_params=pltpu.CompilerParams(
+            collective_id=1, has_side_effects=True, vmem_limit_bytes=52 * 1024 * 1024
+        ),
+        cost_estimate=pl.CostEstimate(
+            flops=2 * rows * width * depth,
+            bytes_accessed=2 * width * depth + 4 * rows * width,
+            transcendentals=0,
+        ),
+        name="norm_project_reduce",
+    )(gated, part, live, member, gain, w_out)
 
 
 def scan_kernel(
@@ -404,34 +746,30 @@
     local_x = w_in_x.shape[1]
     local_bc = w_in_bc.shape[1]
     local_heads = w_in_dt.shape[1]
-    flat_rows = lax.all_gather(suffix_acts, "tensor", axis=1, tiled=True)[0]
+    flat_rows, raw_x, raw_bc, raw_dt = project_call(suffix_acts[0], w_in_x, w_in_bc, w_in_dt)
     seq_len = flat_rows.shape[0] // requests
-    raw_bc = jnp.dot(flat_rows, w_in_bc, preferred_element_type=jnp.float32)
-    raw_bc = raw_bc.astype(jnp.bfloat16).reshape(requests, seq_len, local_bc)
+    raw_bc = raw_bc.reshape(requests, seq_len, local_bc)
     ext_bc, act_bc = causal_conv(tail_bc, raw_bc, conv_bc)
     every_bc = lax.all_gather(
         act_bc.reshape(requests * seq_len, local_bc), "tensor", axis=1, tiled=True
     )
-    raw_x = jnp.dot(flat_rows, w_in_x, preferred_element_type=jnp.float32).astype(jnp.bfloat16)
     raw_z = jnp.dot(flat_rows, w_in_z, preferred_element_type=jnp.float32).astype(jnp.bfloat16)
-    raw_dt = jnp.dot(flat_rows, w_in_dt, preferred_element_type=jnp.float32)
     dt = raw_dt.reshape(requests, seq_len, local_heads)
     new_tail_bc = last_rows(ext_bc, lengths)
     gated, part, new_states, new_tail_x = scan_call(
         slot, mine.astype(jnp.int32), lengths, raw_x, raw_z, dt, dt.transpose(0, 2, 1), every_bc,
         cache_conv_x, got_x, cache_states, got_state, conv_x, dt_bias, decay_rate, skip_gain,
     )
-    total = lax.psum(part, "tensor")
-    inverse = lax.rsqrt(total / (HEADS // GROUPS * HDIM) + epsilon)
     live = jnp.arange(seq_len, dtype=jnp.int32)[None, :] < lengths[:, None]
-    inverse = jnp.where(live.reshape(-1)[:, None], inverse, 0.0)
-    inverse = jnp.repeat(jnp.tile(inverse, (1, local_heads // GROUPS)), HDIM, axis=1)
-    normed = (gated * inverse * norm_gain).astype(jnp.bfloat16)
-    mixed_out = lax.psum_scatter(
-        jnp.dot(normed, w_out, preferred_element_type=jnp.float32).astype(jnp.bfloat16),
-        "tensor",
-        scatter_dimension=0,
-        tiled=True,
+    channel = jnp.arange(local_x, dtype=jnp.int32) // HDIM % GROUPS
+    member = (jnp.arange(16, dtype=jnp.int32) % 8)[:, None] == channel[None, :]
+    mixed_out = output_call(
+        gated,
+        jnp.pad(part.T, ((0, 8 - GROUPS), (0, 0))),
+        live.astype(jnp.float32).reshape(1, -1),
+        member.astype(jnp.bfloat16),
+        norm_gain[None],
+        w_out,
     )
     return (
         mixed_out[None],

time: 371 us -> 286 us (0.77)
  waiting for transfers between devices: 223 us -> 24.6 us
  Pallas kernels: 20.1 us -> 184 us
  blocking collectives: 38.8 us -> 0 us
  matrix products: 43.9 us -> 11 us
  local copies, waits for them, and re-layouts: 27.5 us -> 43.9 us
    pallas_call x0 -> x2, Pallas kernels: none -> 164 us  [the longest x1 82.9 us: project_call(): pl.pallas_call(project_kernel, in_specs=[hbm] * 4, out_specs=[hbm, vmem,...]
    reduce_scatter x1 -> x0, waiting for transfers between devices: 114 us -> none  [local(): lax.psum_scatter(jnp.dot(normed, w_out, preferred_element_type=jnp.float3...]
    all_gather x1 -> x0, waiting for transfers between devices: 91.3 us -> none  [local(): flat_rows = lax.all_gather(suffix_acts, 'tensor', axis=1, tiled=True)[0]]
    psum x1 -> x0, blocking collectives: 38.8 us -> none  [local(): total = lax.psum(part, 'tensor')]
    dot_general x4 -> x0, matrix products: 32.9 us -> none  [the longest x1 13 us: local(): jnp.dot(normed, w_out, preferred_element_type=jnp.float32)]
    unnamed x41 -> x73, local copies, waits for them, and re-layouts: 9.35 us -> 24.9 us
    all_gather x1, waiting for transfers between devices: 16.9 us -> 24.6 us  [local(): lax.all_gather(act_bc.reshape(requests * seq_len, local_bc), 'tensor', ax...]
  transfers between devices with their start and end apart: 6 -> 4, of which waited for: 3 -> 1; matrix products, arithmetic and copies ran while one was open for 13% -> 12% of each run, Pallas kernels for 0% -> 29%
where the time goes in v2:
time: 286 us; the launch traced here: 285 us
  Pallas kernels  184 us (64%)
  local copies, waits for them, and re-layouts  43.9 us (15%)
  waiting for transfers between devices  24.6 us (9%)
  between operations  14.3 us (5%)
  matrix products  11 us (4%)
  other arithmetic  5.22 us (2%)
    pallas_call x1, Pallas kernels, project_call(): pl.pallas_call(project_kernel, in_specs=[hbm] * 4, out_specs=[hbm, vmem,...  82.9 us
    pallas_call x1, Pallas kernels, output_call(): pl.pallas_call(output_kernel, in_specs=[vmem] * 5 + [pl.BlockSpec(memory_...  81.4 us
    unnamed x73, local copies, waits for them, and re-layouts  24.9 us
    all_gather x1, waiting for transfers between devices, local(): lax.all_gather(act_bc.reshape(requests * seq_len, local_bc), 'tensor', ax...  24.6 us
    pallas_call x1, Pallas kernels, scan_call(): pl.pallas_call(scan_kernel, grid_spec=pltpu.PrefetchScalarGridSpec(num_sc...  20.2 us
    dot_general x1, matrix products, local(): jnp.dot(flat_rows, w_in_z, preferred_element_type=jnp.float32)  11 us
    gather x1, local copies, waits for them, and re-layouts, local(): cache_states[other_slot].astype(jnp.bfloat16)  6.36 us
  transfers between devices with their start and end apart: 4, of which 1 were waited for; matrix products, arithmetic and copies ran while one was open for 12% of the time, Pallas kernels for 29%

profile of v2, /device:TPU:0, one launch (start us, length us, event | category | flops | bytes accessed | tf_op | source)
XLA Modules:
  0.0 284.5 jit_solution(3549425673421406986)
XLA Ops:
  7.2 0.0 copy-start
  7.2 0.0 all-gather.2.cloned.1.call-start
  7.3 1.3 fusion.15
  8.6 0.6 gather_fusion.1
  9.2 0.5 collective-permute-start
  9.7 1.7 gather_fusion.2
  11.5 0.7 copy.39
  12.2 0.1 collective-permute-start.1
  12.3 6.4 %gather_fusion.3 = bf16[16,16,64,128]{3,2,1,0:T(8,128)(2,1)} fusion(f32[16,16,64,128]{3,2,1,0:T(8,128)} %own_state_ref.1, s32[1024]{0:T(1024)S(1)} %pad_clamp_fusion), kind=kCustom, calls=%fused_computation.3 | custom fusion | bytes 8388672 | tf_op jit(solution)/shard_map/gather | solution.py:744
  18.6 0.5 collective-permute-start.2
  19.1 0.1 fusion.5
  19.2 0.5 copy.33.w_dt_ref
  19.7 0.6 fusion.17
  20.3 1.2 copy-done.21
  21.5 1.1 copy-done.22
  22.7 82.9 %gather_project.1 = (bf16[768,4096]{1,0:T(8,128)(2,1)S(1)}, bf16[768,1024]{1,0:T(8,128)(2,1)S(1)}, bf16[768,128]{1,0:T(8,128)(2,1)S(1)}, f32[768,16]{1,0:T(8,128)S(1)}) custom-call(bf16[96,4096]{1,0:T(8,128)(2,1)S(1)} %bitcast.58, bf16[4096,1024]{1,0:T(8,128)(2,1)} %w_x_ref.1, bf16[4096,128]{1,0:T(8,128)(2,1)S(1)} %copy-done.21, ...), custom_call_target="tpu_custom_call" | custom-call | flops 6442450944 | bytes 20971520 | tf_op jit(solution)/shard_map/gather_project/pallas_call | solution.py:307
  105.5 0.0 copy-start.24
  105.5 2.7 copy-done.24
  108.2 0.7 copy.41.own_x_ref
  109.0 0.6 gather_fusion
  109.6 0.6 reshape.262
  110.2 0.1 copy.36
  110.3 0.1 broadcast_select_fusion.1
  110.4 0.6 copy-done.26
  110.9 0.2 multiply_convert_fusion
  111.1 0.7 copy.38
  111.9 0.0 all-gather.2.cloned.1.call-update
  111.9 0.1 fusion.9
  112.0 0.7 reshape.229.live_ref
  112.7 0.1 broadcast_in_dim.59
  112.7 0.1 broadcast_in_dim_reshape.3.skip_ref
  112.8 0.7 copy.43.decay_t_ref
  113.5 0.1 copy.42.bias_t_ref
  113.6 0.8 copy.35
  114.4 0.7 fusion.8
  115.0 0.7 compare_convert_fusion.member_ref
  115.7 11.0 %convolution_convert_fusion.raw_z_ref = bf16[768,1024]{1,0:T(8,128)(2,1)S(1)} fusion(bf16[768,4096]{1,0:T(8,128)(2,1)} %copy-done.24, bf16[4096,1024]{1,0:T(8,128)(2,1)} %param.26), kind=kOutput, calls=%fused_computation.5 | convolution fusion | flops 6443237376 | bytes 16252928 | tf_op jit(solution)/shard_map/dot_general | solution.py:756
  126.8 0.7 pad_maximum_fusion
  127.5 2.7 gather_fusion.4
  130.1 1.3 gather.23
  131.4 0.8 broadcast_select_fusion
  132.3 0.6 copy.46
  132.9 24.6 %all-gather.2.cloned.1.call-done.bc_ref = bf16[768,1024]{1,0:T(8,128)(2,1)} async-done(((bf16[768,128]{1,0:T(8,128)(2,1)}), bf16[768,1024]{1,0:T(8,128)(2,1)}) %all-gather.2.cloned.1.call-update) | async-done | bytes 1572880 | tf_op jit(solution)/shard_map/all_gather | solution.py:753
  157.5 3.4 %copy-done.2 = f32[16,16,64,128]{3,2,1,0:T(8,128)S(1)} copy-done((f32[16,16,64,128]{3,2,1,0:T(8,128)S(1)}, f32[16,16,64,128]{3,2,1,0:T(8,128)}, u32[]{:S(2)}) %copy-start.2) | copy-done | bytes 8388632
  160.9 1.4 copy-done.3
  162.3 0.9 copy-done.4
  163.2 0.9 copy-done.5
  164.1 0.7 copy-done.9
  164.8 0.7 copy-done.11
  165.5 0.7 copy-done.15
  166.1 0.7 copy-done.17
  166.8 0.7 copy-done.18
  167.5 0.7 copy-done.19
  168.1 20.2 %scan.1 = (f32[768,1024]{1,0:T(8,128)S(1)}, f32[768,4]{1,0:T(8,128)S(1)}, f32[16,16,64,128]{3,2,1,0:T(8,128)}, bf16[16,3,1024]{2,1,0:T(4,128)(2,1)S(1)}) custom-call(s32[16]{0:T(128)S(1)} %bitcast.57, s32[16]{0:T(128)S(1)} %copy-done.19, s32[16]{0:T(128)S(1)} %bitcast.52, bf16[768,1024]{1,0:T(8,128)(2,1)S(1)} %get-tuple-element.12.raw_x_ref, ...), custom_call_target="tpu_custom_call" | custom-call | flops 478150656 | bytes 20971520 | tf_op jit(solution)/shard_map/scan/pallas_call | solution.py:665
  188.4 0.7 copy-done.6
  189.1 0.6 copy-done.7
  189.8 1.6 copy-done.20
  191.4 1.1 copy.44
  192.6 0.8 copy-done.10
  193.3 0.7 copy-done.13
  194.0 0.7 copy-done.23
  194.7 81.4 %norm_project_reduce.1 = bf16[96,4096]{1,0:T(8,128)(2,1)S(1)} custom-call(f32[768,1024]{1,0:T(8,128)} %copy-done.20, f32[8,768]{1,0:T(8,128)S(1)} %pad.4.part_ref, f32[1,768]{1,0:T(1,128)S(1)} %copy-done.13, bf16[16,1024]{1,0:T(8,128)(2,1)S(1)} %copy-done.10, f32[1,1024]{1,0:T(1,128)S(1)} %bitcast.59, bf16[1024,4096]{1,0:T(8,128)(2,1)} %w_ref.1), custom_call_target="tpu_custom_call" | custom-call | flops 6442450944 | bytes 11534336 | tf_op jit(solution)/shard_map/norm_project_reduce/pallas_call | solution.py:469
  276.1 0.7 copy.45
  276.8 0.9 copy.50
  (55 shorter events, 0.1 us)
Async XLA Ops:
  7.2 1.5 copy-start
  7.2 11.9 %copy-start.31 = (f32[4,128]{1,0:T(4,128)S(1)}, f32[4,128]{1,0:T(4,128)}, u32[]{:S(2)}) copy-start(f32[4,128]{1,0:T(4,128)} %param.30) | copy-start | bytes 6148
  7.2 11.9 %copy-start.12 = (s32[1,16]{1,0:T(1,128)S(1)}, s32[1,16]{1,0:T(1,128)}, u32[]{:S(2)}) copy-start(s32[1,16]{1,0:T(1,128)} %param.19) | copy-start | bytes 196
  7.2 12.0 %copy-start.28 = (bf16[4096,16]{0,1:T(8,128)(2,1)S(1)}, bf16[4096,16]{0,1:T(8,128)(2,1)}, u32[]{:S(2)}) copy-start(bf16[4096,16]{0,1:T(8,128)(2,1)} %param.28) | copy-start | bytes 393220
  7.2 12.5 %copy-start.32 = (s32[2,16]{1,0:T(2,128)S(1)}, s32[2,16]{1,0:T(2,128)}, u32[]{:S(2)}) copy-start(s32[2,16]{1,0:T(2,128)} %param.20) | copy-start | bytes 388
  7.2 150.2 %all-gather.2.cloned.1.call-start = ((), (), s32[]{:S(2)}) async-start(), calls=%async_computation | async-start | bytes 1769472 | tf_op jit(solution)/shard_map/all_gather | solution.py:753
  9.2 101.0 %collective-permute-start = (bf16[16,3,128]{2,0,1:T(8,128)(2,1)S(1)}, bf16[16,3,128]{2,0,1:T(8,128)(2,1)S(1)}, u32[]{:S(2)}, u32[]{:S(2)}) collective-permute-start(bf16[16,3,128]{2,0,1:T(8,128)(2,1)S(1)} %gather_fusion.1), channel_id=1, source_target_pairs={{0,8},{8,0},{1,9},{9,1},{2,10},{10,2},{3,11},{11,3},{4,12},{12,4},... | collective-permute-start | bytes 36872 | tf_op jit(solution)/shard_map/ppermute | solution.py:742
  12.2 120.6 %collective-permute-start.1 = (bf16[16,3,1024]{2,1,0:T(4,128)(2,1)}, bf16[16,3,1024]{2,1,0:T(4,128)(2,1)}, u32[]{:S(2)}, u32[]{:S(2)}) collective-permute-start(bf16[16,3,1024]{2,1,0:T(4,128)(2,1)} %copy.39), channel_id=1, source_target_pairs={{0,8},{8,0},{1,9},{9,1},{2,10},{10,2},{3,11},{11,3},{4,12},{12,4},... | collective-permute-start | bytes 294920 | tf_op jit(solution)/shard_map/ppermute | solution.py:743
  18.6 138.8 %collective-permute-start.2 = (bf16[16,16,64,128]{3,2,1,0:T(8,128)(2,1)}, bf16[16,16,64,128]{3,2,1,0:T(8,128)(2,1)}, u32[]{:S(2)}, u32[]{:S(2)}) collective-permute-start(bf16[16,16,64,128]{3,2,1,0:T(8,128)(2,1)} %gather_fusion.3), channel_id=1, source_target_pairs={{0,8},{8,0},{1,9},{9,1},{2,10},{10,2},{3,11},{11,3},{4,12},{12,4},... | collective-permute-start | bytes 12582920 | tf_op jit(solution)/shard_map/ppermute | solution.py:744
  20.3 1.2 copy-start.21
  21.5 1.1 copy-start.22
  22.6 85.6 %copy-start.25 = (bf16[16,3,1024]{2,0,1:T(8,128)(2,1)S(1)}, bf16[16,3,1024]{2,0,1:T(8,128)(2,1)}, u32[]{:S(2)}) copy-start(bf16[16,3,1024]{2,0,1:T(8,128)(2,1)} %param.23) | copy-start | bytes 294916
  22.6 90.0 %copy-start.33 = (f32[16]{0:T(128)S(1)}, f32[16]{0:T(128)}, u32[]{:S(2)}) copy-start(f32[16]{0:T(128)} %param.33) | copy-start | bytes 196
  22.6 90.2 %copy-start.16 = (f32[16]{0:T(128)S(1)}, f32[16]{0:T(128)}, u32[]{:S(2)}) copy-start(f32[16]{0:T(128)} %param.32) | copy-start | bytes 196
  22.6 90.8 %copy-start.14 = (f32[16]{0:T(128)S(1)}, f32[16]{0:T(128)}, u32[]{:S(2)}) copy-start(f32[16]{0:T(128)} %param.31) | copy-start | bytes 196
  105.5 2.7 copy-start.24
  110.3 0.7 copy-start.26
  110.4 2.3 copy-start.29
  115.7 11.0 %copy-start.27 = (bf16[16,48,128]{2,0,1:T(8,128)(2,1)S(1)}, bf16[16,48,128]{2,0,1:T(8,128)(2,1)}, u32[]{:S(2)}) copy-start(bf16[16,48,128]{2,0,1:T(8,128)(2,1)} %copy-done.26) | copy-start | bytes 589828
  115.7 11.0 %copy-start.30 = (bf16[16,3,128]{2,0,1:T(8,128)(2,1)S(1)}, bf16[16,3,128]{2,0,1:T(8,128)(2,1)}, u32[]{:S(2)}) copy-start(bf16[16,3,128]{2,0,1:T(8,128)(2,1)} %copy-done.29) | copy-start | bytes 36868
  157.5 3.4 %copy-start.2 = (f32[16,16,64,128]{3,2,1,0:T(8,128)S(1)}, f32[16,16,64,128]{3,2,1,0:T(8,128)}, u32[]{:S(2)}) copy-start(f32[16,16,64,128]{3,2,1,0:T(8,128)} %own_state_ref.1) | copy-start | bytes 25165828
  160.9 1.4 copy-start.3
  162.3 0.9 copy-start.4
  163.2 0.9 copy-start.5
  164.1 0.7 copy-start.9
  164.8 0.7 copy-start.11
  165.5 0.7 copy-start.15
  166.1 0.7 copy-start.17
  166.8 0.7 copy-start.18
  167.5 0.7 copy-start.19
  188.4 0.7 copy-start.6
  189.1 0.6 copy-start.7
  189.8 1.6 copy-start.20
  192.5 0.8 copy-start.10
  193.3 0.7 copy-start.13
  194.0 0.7 copy-start.23
  194.7 81.4 %copy-start.8 = (bf16[16,3,1024]{2,1,0:T(4,128)(2,1)S(1)}, bf16[16,3,1024]{2,1,0:T(4,128)(2,1)}, u32[]{:S(2)}) copy-start(bf16[16,3,1024]{2,1,0:T(4,128)(2,1)} %copy-done.7) | copy-start | bytes 294916
  194.7 83.0 %copy-start.1 = (bf16[16,3,128]{2,0,1:T(8,128)(2,1)S(1)}, bf16[16,3,128]{2,0,1:T(8,128)(2,1)}, u32[]{:S(2)}) copy-start(bf16[16,3,128]{2,0,1:T(8,128)(2,1)} %param.24) | copy-start | bytes 36868
Sparse Core Ops, SparseCore 0:
  112.0 45.4 all-gather.1

commit v3 on v2

--- a/solution.py
+++ b/solution.py
@@ -338,6 +338,133 @@
     )(acts, w_x, w_bc, w_dt)
 
 
+def gate_kernel(
+    bc_ref, rows_ref, w_ref, every_ref, z_ref,
+    held, rows_buf, w_buf, load_sem, store_sem, line_send, line_recv, side_send, side_recv,
+):
+    me, z, y = place()
+    side = me + 1 - 2 * y
+    loads = [
+        pltpu.make_async_copy(bc_ref, held.at[me], load_sem.at[0]),
+        pltpu.make_async_copy(w_ref, w_buf, load_sem.at[1]),
+        pltpu.make_async_copy(rows_ref, rows_buf, load_sem.at[2]),
+    ]
+    for load in loads:
+        load.start()
+    signal(side)
+
+    @pl.when(z < LINE - 1)
+    def _():
+        signal(me + 2)
+
+    @pl.when(z > 0)
+    def _():
+        signal(me - 2)
+
+    ends = (z == 0) | (z == LINE - 1)
+    pl.semaphore_wait(pltpu.get_barrier_semaphore(), jnp.where(ends, 2, 3))
+
+    def spot(plane, column):
+        return held.at[2 * plane + column]
+
+    def up(plane):
+        return remote(
+            spot(plane, y), spot(plane, y), line_send.at[0, plane], line_recv.at[plane], me + 2
+        )
+
+    def down(plane):
+        return remote(
+            spot(plane, y), spot(plane, y), line_send.at[1, plane], line_recv.at[plane], me - 2
+        )
+
+    def across(plane):
+        return remote(
+            spot(plane, y), spot(plane, y), side_send.at[plane], side_recv.at[plane], side
+        )
+
+    def arrived(plane, column, sem):
+        return remote(spot(plane, column), spot(plane, column), line_send.at[0, 0], sem, side)
+
+    loads[0].wait()
+    for k in range(LINE + 1):
+        if k < LINE:
+            plane = nearest(z, k)
+            if k > 0:
+                arrived(plane, y, line_recv.at[plane]).wait_recv()
+
+            @pl.when((plane <= z) & (z < LINE - 1))
+            def _():
+                up(plane).start()
+
+            @pl.when((plane >= z) & (z > 0))
+            def _():
+                down(plane).start()
+
+            across(plane).start()
+        if k == 1:
+            for load in loads[1:]:
+                load.wait()
+        if k > 0:
+            share = rows_buf.shape[0] // LINE
+            span = slice((k - 1) * share, k * share)
+            tile = 256
+
+            def step(j, carry):
+                columns = pl.ds(pl.multiple_of(j * tile, tile), tile)
+                z_ref[span, columns] = jnp.dot(
+                    rows_buf[span, :], w_buf[:, columns], preferred_element_type=jnp.float32
+                ).astype(jnp.bfloat16)
+                return carry
+
+            lax.fori_loop(0, z_ref.shape[1] // tile, step, 0)
+    for k in range(LINE):
+        plane = nearest(z, k)
+
+        @pl.when((plane <= z) & (z < LINE - 1))
+        def _():
+            up(plane).wait_send()
+
+        @pl.when((plane >= z) & (z > 0))
+        def _():
+            down(plane).wait_send()
+
+        across(plane).wait_send()
+        arrived(plane, 1 - y, side_recv.at[plane]).wait_recv()
+    store = pltpu.make_async_copy(held, every_ref, store_sem)
+    store.start()
+    store.wait()
+
+
+def gate_call(bc, flat_rows, w_z):
+    rows, depth = flat_rows.shape
+    hbm = pl.BlockSpec(memory_space=pl.ANY)
+    dma = pltpu.SemaphoreType.DMA
+    return pl.pallas_call(
+        gate_kernel,
+        in_specs=[hbm] * 3,
+        out_specs=[hbm, pl.BlockSpec(memory_space=pltpu.VMEM)],
+        out_shape=[
+            jax.ShapeDtypeStruct((2 * LINE, *bc.shape), jnp.bfloat16),
+            jax.ShapeDtypeStruct((rows, w_z.shape[1]), jnp.bfloat16),
+        ],
+        scratch_shapes=[
+            pltpu.VMEM((2 * LINE, *bc.shape), jnp.bfloat16),
+            pltpu.VMEM(flat_rows.shape, jnp.bfloat16),
+            pltpu.VMEM(w_z.shape, jnp.bfloat16),
+            dma((3,)),
+            dma,
+            dma((2, LINE)),
+            dma((LINE,)),
+            dma((LINE,)),
+            dma((LINE,)),
+        ],
+        compiler_params=pltpu.CompilerParams(
+            collective_id=2, has_side_effects=True, vmem_limit_bytes=40 * 1024 * 1024
+        ),
+        name="gather_gate",
+    )(bc, flat_rows, w_z)
+
+
 def output_kernel(
     gated_ref, part_ref, live_ref, member_ref, gain_ref, w_ref, out_ref,
     parts, normed, w_buf, own, side_out, side_in, line_out, line_in,
@@ -571,11 +698,10 @@
         precision=highest,
         preferred_element_type=jnp.float32,
     )
-    half = GROUPS * NSTATE
     contract_last = (((1,), (1,)), ((), ()))
     contract_first = (((0,), (0,)), ((), ()))
-    b_rows = [bc_ref[:, g * NSTATE : (g + 1) * NSTATE] for g in range(GROUPS)]
-    c_rows = [bc_ref[:, half + g * NSTATE : half + (g + 1) * NSTATE] for g in range(GROUPS)]
+    b_rows = [bc_ref[g] for g in range(GROUPS)]
+    c_rows = [bc_ref[GROUPS + g] for g in range(GROUPS)]
     scores = [
         lax.dot_general(
             c_rows[g], b_rows[g], contract_last, preferred_element_type=jnp.float32
@@ -672,7 +798,7 @@
                 row(width),
                 by_q(seq, heads),
                 by_q(heads, seq),
-                row(every_bc.shape[1]),
+                pl.BlockSpec((every_bc.shape[0], seq, NSTATE), lambda q, *_: (0, q, 0)),
                 by_slot(KT, width),
                 by_q(KT, width),
                 by_slot(heads, HDIM, NSTATE),
@@ -750,10 +876,9 @@
     seq_len = flat_rows.shape[0] // requests
     raw_bc = raw_bc.reshape(requests, seq_len, local_bc)
     ext_bc, act_bc = causal_conv(tail_bc, raw_bc, conv_bc)
-    every_bc = lax.all_gather(
-        act_bc.reshape(requests * seq_len, local_bc), "tensor", axis=1, tiled=True
-    )
-    raw_z = jnp.dot(flat_rows, w_in_z, preferred_element_type=jnp.float32).astype(jnp.bfloat16)
+    every_bc, raw_z = gate_call(
+        act_bc.reshape(requests * seq_len, local_bc), flat_rows, w_in_z
+    )
     dt = raw_dt.reshape(requests, seq_len, local_heads)
     new_tail_bc = last_rows(ext_bc, lengths)
     gated, part, new_states, new_tail_x = scan_call(

time: 286 us -> 239 us (0.84)
  waiting for transfers between devices: 24.6 us -> 0.01 us
  Pallas kernels: 184 us -> 205 us
  local copies, waits for them, and re-layouts: 43.9 us -> 27.1 us
  between operations: 14.3 us -> 0.94 us
  matrix products: 11 us -> 0 us
    all_gather x1 -> x0, waiting for transfers between devices: 24.6 us -> none  [local(): lax.all_gather(act_bc.reshape(requests * seq_len, local_bc), 'tensor', ax...]
    pallas_call x0 -> x1, Pallas kernels: none -> 24.2 us  [gate_call(): pl.pallas_call(gate_kernel, in_specs=[hbm] * 3, out_specs=[hbm, pl.BlockS...]
    unnamed x73 -> x49, local copies, waits for them, and re-layouts: 24.9 us -> 12.7 us
    dot_general x1 -> x0, matrix products: 11 us -> none  [local(): jnp.dot(flat_rows, w_in_z, preferred_element_type=jnp.float32)]
    pallas_call x1, Pallas kernels: 81.4 us -> 78.1 us  [output_call(): pl.pallas_call(output_kernel, in_specs=[vmem] * 5 + [pl.BlockSpec(memory_...]
  transfers between devices with their start and end apart: 4 -> 3, of which waited for: 1 -> 0; matrix products, arithmetic and copies ran while one was open for 12% -> 5% of each run, Pallas kernels for 29% -> 45%
where the time goes in v3:
time: 239 us; the launch traced here: 238 us
  Pallas kernels  205 us (86%)
  local copies, waits for them, and re-layouts  27.1 us (11%)
  other arithmetic  4.05 us (2%)
    pallas_call x1, Pallas kernels, project_call(): pl.pallas_call(project_kernel, in_specs=[hbm] * 4, out_specs=[hbm, vmem,...  82.9 us
    pallas_call x1, Pallas kernels, output_call(): pl.pallas_call(output_kernel, in_specs=[vmem] * 5 + [pl.BlockSpec(memory_...  78.1 us
    pallas_call x1, Pallas kernels, gate_call(): pl.pallas_call(gate_kernel, in_specs=[hbm] * 3, out_specs=[hbm, pl.BlockS...  24.2 us
    pallas_call x1, Pallas kernels, scan_call(): pl.pallas_call(scan_kernel, grid_spec=pltpu.PrefetchScalarGridSpec(num_sc...  20.1 us
    unnamed x49, local copies, waits for them, and re-layouts  12.7 us
    gather x1, local copies, waits for them, and re-layouts, local(): cache_states[other_slot].astype(jnp.bfloat16)  6.44 us
  transfers between devices with their start and end apart: 3, of which 0 were waited for; matrix products, arithmetic and copies ran while one was open for 5% of the time, Pallas kernels for 45%

profile of v3, /device:TPU:0, one launch (start us, length us, event | category | flops | bytes accessed | tf_op | source)
XLA Modules:
  0.0 238.3 jit_solution(9462337850271803011)
XLA Ops:
  0.6 0.0 copy-start
  0.7 0.8 fusion.15
  1.4 0.0 copy-start.15
  1.4 0.0 copy-start.17
  1.4 0.0 copy-start.19
  1.5 0.0 copy-start.8
  1.5 0.0 copy-start.18
  1.5 6.4 %gather_fusion.3 = bf16[16,16,64,128]{3,2,1,0:T(8,128)(2,1)} fusion(f32[16,16,64,128]{3,2,1,0:T(8,128)} %own_state_ref.1, s32[1024]{0:T(1024)S(1)} %pad_clamp_fusion), kind=kCustom, calls=%fused_computation.3 | custom fusion | bytes 8388672 | tf_op jit(solution)/shard_map/gather | solution.py:870
  7.9 0.5 collective-permute-start.2
  8.4 0.0 copy-done
  8.4 1.2 gather_fusion.1
  9.6 0.1 collective-permute-start
  9.6 0.0 copy-done.15
  9.6 0.8 gather_fusion.2
  10.5 0.7 copy.39
  11.2 0.5 collective-permute-start.1
  11.7 0.0 copy-done.17
  11.7 0.6 copy.33.w_dt_ref
  12.3 0.0 copy-done.19
  12.3 0.6 fusion.17
  12.9 0.0 copy-done.8
  12.9 0.1 fusion.8
  13.0 0.0 copy-done.18
  13.0 0.6 slice_bitcast_fusion.3
  13.6 0.7 fusion.5
  14.3 0.1 fusion.9
  14.3 0.1 compare_convert_fusion.member_ref
  14.4 1.2 copy-done.12
  15.6 1.1 copy-done.13
  16.8 82.9 %gather_project.1 = (bf16[768,4096]{1,0:T(8,128)(2,1)S(1)}, bf16[768,1024]{1,0:T(8,128)(2,1)S(1)}, bf16[768,128]{1,0:T(8,128)(2,1)S(1)}, f32[768,16]{1,0:T(8,128)S(1)}) custom-call(bf16[96,4096]{1,0:T(8,128)(2,1)S(1)} %bitcast.59, bf16[4096,1024]{1,0:T(8,128)(2,1)} %w_x_ref.1, bf16[4096,128]{1,0:T(8,128)(2,1)S(1)} %copy-done.12, ...), custom_call_target="tpu_custom_call" | custom-call | flops 6442450944 | bytes 20971520 | tf_op jit(solution)/shard_map/gather_project/pallas_call | solution.py:307
  99.7 0.0 copy-start.2
  99.7 2.7 %copy-done.2 = bf16[768,4096]{1,0:T(8,128)(2,1)} copy-done((bf16[768,4096]{1,0:T(8,128)(2,1)}, bf16[768,4096]{1,0:T(8,128)(2,1)S(1)}, u32[]{:S(2)}) %copy-start.2) | copy-done | bytes 6291480
  102.4 0.1 copy.41.own_x_ref
  102.5 0.6 gather_fusion
  103.1 0.8 reshape.262
  103.9 0.1 reshape.229.live_ref
  104.0 0.7 broadcast_in_dim.59
  104.7 0.1 broadcast_in_dim_reshape.3.skip_ref
  104.8 0.1 copy.43.decay_t_ref
  104.9 0.0 copy-done.9
  104.9 0.1 copy.42.bias_t_ref
  104.9 0.1 copy.34
  105.0 0.8 copy.38
  105.8 0.0 collective-permute-done
  105.8 0.8 broadcast_select_fusion.1
  106.6 1.0 gather_fusion.4
  107.7 0.9 multiply_convert_fusion
  108.5 0.1 broadcast_select_fusion
  108.6 0.0 slice-start
  108.6 0.1 copy.36
  108.7 0.6 copy.46
  109.3 3.1 %copy-done.3 = bf16[768,4096]{1,0:T(8,128)(2,1)S(1)} copy-done((bf16[768,4096]{1,0:T(8,128)(2,1)S(1)}, bf16[768,4096]{1,0:T(8,128)(2,1)}, u32[]{:S(2)}) %copy-start.3) | copy-done | bytes 6291480
  112.4 24.2 %gather_gate.1 = (bf16[8,768,128]{2,1,0:T(8,128)(2,1)S(1)}, bf16[768,1024]{1,0:T(8,128)(2,1)S(1)}) custom-call(bf16[768,128]{1,0:T(8,128)(2,1)S(1)} %bitcast.45, bf16[768,4096]{1,0:T(8,128)(2,1)S(1)} %copy-done.3, bf16[4096,1024]{1,0:T(8,128)(2,1)} %w_ref.2), custom_call_target="tpu_custom_call" | custom-call | tf_op jit(solution)/shard_map/gather_gate/pallas_call | solution.py:442
  136.6 0.0 collective-permute-done.1.got_x_ref
  136.6 0.0 collective-permute-done.2.got_state_ref
  136.7 0.0 copy-start.14
  136.7 20.1 %scan.1 = (f32[768,1024]{1,0:T(8,128)S(1)}, f32[768,4]{1,0:T(8,128)S(1)}, f32[16,16,64,128]{3,2,1,0:T(8,128)}, bf16[16,3,1024]{2,1,0:T(4,128)(2,1)S(1)}) custom-call(s32[16]{0:T(128)S(1)} %bitcast.58, s32[16]{0:T(128)S(1)} %get-tuple-element.34.mine_ref, s32[16]{0:T(128)S(1)} %bitcast.53, bf16[768,1024]{1,0:T(8,128)(2,1)S(1)} %get-tuple-element.14.raw_x_ref, ...), custom_call_target="tpu_custom_call" | custom-call | flops 478150656 | bytes 20971520 | tf_op jit(solution)/shard_map/scan/pallas_call | solution.py:791
  156.8 1.6 copy-done.11
  158.4 0.1 copy.44
  158.6 0.0 copy-done.14
  158.6 0.0 copy-start.1
  158.6 78.1 %norm_project_reduce.1 = bf16[96,4096]{1,0:T(8,128)(2,1)S(1)} custom-call(f32[768,1024]{1,0:T(8,128)} %copy-done.11, f32[8,768]{1,0:T(8,128)S(1)} %pad.4.part_ref, f32[1,768]{1,0:T(1,128)S(1)} %reshape.229.live_ref, bf16[16,1024]{1,0:T(8,128)(2,1)S(1)} %compare_convert_fusion.member_ref, f32[1,1024]{1,0:T(1,128)S(1)} %bitcast.60, bf16[1024,4096]{1,0:T(8,128)(2,1)} %w_ref.3), custom_call_target="tpu_custom_call" | custom-call | flops 6442450944 | bytes 11534336 | tf_op jit(solution)/shard_map/norm_project_reduce/pallas_call | solution.py:596
  236.7 0.7 copy.45
  237.4 0.9 copy.50
  (29 shorter events, 0.1 us)
Async XLA Ops:
  0.6 7.8 %copy-start = (bf16[16,3,128]{2,0,1:T(8,128)(2,1)S(1)}, bf16[16,3,128]{2,0,1:T(8,128)(2,1)}, u32[]{:S(2)}) copy-start(bf16[16,3,128]{2,0,1:T(8,128)(2,1)} %param.24) | copy-start | bytes 36868
  1.4 8.2 %copy-start.15 = (bf16[16,3,1024]{2,0,1:T(8,128)(2,1)S(1)}, bf16[16,3,1024]{2,0,1:T(8,128)(2,1)}, u32[]{:S(2)}) copy-start(bf16[16,3,1024]{2,0,1:T(8,128)(2,1)} %param.23) | copy-start | bytes 294916
  1.4 10.3 %copy-start.17 = (bf16[4096,16]{0,1:T(8,128)(2,1)S(1)}, bf16[4096,16]{0,1:T(8,128)(2,1)}, u32[]{:S(2)}) copy-start(bf16[4096,16]{0,1:T(8,128)(2,1)} %param.28) | copy-start | bytes 393220
  1.4 10.8 %copy-start.19 = (s32[2,16]{1,0:T(2,128)S(1)}, s32[2,16]{1,0:T(2,128)}, u32[]{:S(2)}) copy-start(s32[2,16]{1,0:T(2,128)} %param.20) | copy-start | bytes 388
  1.5 11.4 %copy-start.8 = (s32[1,16]{1,0:T(1,128)S(1)}, s32[1,16]{1,0:T(1,128)}, u32[]{:S(2)}) copy-start(s32[1,16]{1,0:T(1,128)} %param.19) | copy-start | bytes 196
  1.5 11.5 %copy-start.18 = (f32[4,128]{1,0:T(4,128)S(1)}, f32[4,128]{1,0:T(4,128)}, u32[]{:S(2)}) copy-start(f32[4,128]{1,0:T(4,128)} %param.30) | copy-start | bytes 6148
  7.9 128.7 %collective-permute-start.2 = (bf16[16,16,64,128]{3,2,1,0:T(8,128)(2,1)}, bf16[16,16,64,128]{3,2,1,0:T(8,128)(2,1)}, u32[]{:S(2)}, u32[]{:S(2)}) collective-permute-start(bf16[16,16,64,128]{3,2,1,0:T(8,128)(2,1)} %gather_fusion.3), channel_id=1, source_target_pairs={{0,8},{8,0},{1,9},{9,1},{2,10},{10,2},{3,11},{11,3},{4,12},{12,4},... | collective-permute-start | bytes 12582920 | tf_op jit(solution)/shard_map/ppermute | solution.py:870
  9.6 96.2 %collective-permute-start = (bf16[16,3,128]{2,0,1:T(8,128)(2,1)}, bf16[16,3,128]{2,0,1:T(8,128)(2,1)}, u32[]{:S(2)}, u32[]{:S(2)}) collective-permute-start(bf16[16,3,128]{2,0,1:T(8,128)(2,1)} %gather_fusion.1), channel_id=1, source_target_pairs={{0,8},{8,0},{1,9},{9,1},{2,10},{10,2},{3,11},{11,3},{4,12},{12,4},... | collective-permute-start | bytes 36872 | tf_op jit(solution)/shard_map/ppermute | solution.py:868
  11.2 125.4 %collective-permute-start.1 = (bf16[16,3,1024]{2,1,0:T(4,128)(2,1)}, bf16[16,3,1024]{2,1,0:T(4,128)(2,1)S(1)}, u32[]{:S(2)}, u32[]{:S(2)}) collective-permute-start(bf16[16,3,1024]{2,1,0:T(4,128)(2,1)} %copy.39), channel_id=1, source_target_pairs={{0,8},{8,0},{1,9},{9,1},{2,10},{10,2},{3,11},{11,3},{4,12},{12,4},... | collective-permute-start | bytes 294920 | tf_op jit(solution)/shard_map/ppermute | solution.py:869
  14.4 1.2 copy-start.12
  15.6 1.1 copy-start.13
  16.8 85.6 %copy-start.16 = (bf16[16,3,1024]{2,0,1:T(8,128)(2,1)S(1)}, bf16[16,3,1024]{2,0,1:T(8,128)(2,1)}, u32[]{:S(2)}) copy-start(bf16[16,3,1024]{2,0,1:T(8,128)(2,1)} %param.23) | copy-start | bytes 294916
  16.8 88.0 %copy-start.10 = (f32[16]{0:T(128)S(1)}, f32[16]{0:T(128)}, u32[]{:S(2)}) copy-start(f32[16]{0:T(128)} %param.32) | copy-start | bytes 196
  16.8 88.1 %copy-start.9 = (f32[16]{0:T(128)S(1)}, f32[16]{0:T(128)}, u32[]{:S(2)}) copy-start(f32[16]{0:T(128)} %param.31) | copy-start | bytes 196
  99.7 2.7 %copy-start.2 = (bf16[768,4096]{1,0:T(8,128)(2,1)}, bf16[768,4096]{1,0:T(8,128)(2,1)S(1)}, u32[]{:S(2)}) copy-start(bf16[768,4096]{1,0:T(8,128)(2,1)S(1)} %get-tuple-element.16.rows_ref) | copy-start | bytes 18874372
  102.4 6.9 %copy-start.4 = (f32[768,16]{1,0:T(8,128)}, f32[768,16]{1,0:T(8,128)S(1)}, u32[]{:S(2)}) copy-start(f32[768,16]{1,0:T(8,128)S(1)} %get-tuple-element.18) | copy-start | bytes 147460
  108.6 28.0 %slice-start = ((s8[8388608]{0:T(1024)(128)(4,1)}), s8[4194304]{0:T(1024)(128)(4,1)S(1)}, s32[]{:S(2)}) async-start(s8[8388608]{0:T(1024)(128)(4,1)} %bitcast.41), calls=%async_computation | async-start | bytes 8388608
  109.3 3.1 %copy-start.3 = (bf16[768,4096]{1,0:T(8,128)(2,1)S(1)}, bf16[768,4096]{1,0:T(8,128)(2,1)}, u32[]{:S(2)}) copy-start(bf16[768,4096]{1,0:T(8,128)(2,1)} %copy-done.2) | copy-start | bytes 18874372
  112.4 24.2 %slice-start.1 = ((s8[8388608]{0:T(1024)(128)(4,1)}), s8[4194304]{0:T(1024)(128)(4,1)S(1)}, s32[]{:S(2)}) async-start(s8[8388608]{0:T(1024)(128)(4,1)} %bitcast.41), calls=%async_computation.1 | async-start | bytes 8388608
  112.4 24.2 %copy-start.5 = (f32[768,16]{1,0:T(8,128)S(1)}, f32[768,16]{1,0:T(8,128)}, u32[]{:S(2)}) copy-start(f32[768,16]{1,0:T(8,128)} %copy-done.4) | copy-start | bytes 147460
  112.4 24.2 %copy-start.6 = (f32[16,48,16]{1,2,0:T(8,128)S(1)}, f32[16,48,16]{1,2,0:T(8,128)}, u32[]{:S(2)}) copy-start(f32[16,48,16]{1,2,0:T(8,128)} %copy.38) | copy-start | bytes 147460
  112.4 24.2 %copy-start.7 = (f32[4,1024]{1,0:T(4,128)S(1)}, f32[4,1024]{1,0:T(4,128)}, u32[]{:S(2)}) copy-start(f32[4,1024]{1,0:T(4,128)} %conv_ref.1) | copy-start | bytes 49156
  136.7 21.9 %copy-start.14 = (f32[1024]{0:T(1024)S(1)}, f32[1024]{0:T(1024)}, u32[]{:S(2)}) copy-start(f32[1024]{0:T(1024)} %param.34) | copy-start | bytes 12292
  156.8 1.6 copy-start.11
  158.6 79.7 %copy-start.1 = (bf16[16,3,128]{2,0,1:T(8,128)(2,1)S(1)}, bf16[16,3,128]{2,0,1:T(8,128)(2,1)}, u32[]{:S(2)}) copy-start(bf16[16,3,128]{2,0,1:T(8,128)(2,1)} %param.24) | copy-start | bytes 36868
